TPU v7x, 32 devices: a whole 2x2x4 slice. The times are simulated.
32 devices in a mesh: band: 4 (over x, core), facet: 8 (over z, y).
Axes of the slice: x: 2, y: 2, z: 4, core: 2. Of those that a mesh axis runs over, the one named last changes fastest.
Arguments:
- coeffs: float32 [4, 8, 256, 256], P('band', 'facet'), may hold values from -6 to 6
- dirty: float32 [16, 8, 256, 256], P('band', 'facet'), may hold values from -6 to 6
- psf: float32 [16, 8, 129, 129], P('band', 'facet'), may hold values from -0.046875 to 0.046875
- band_offset: float32 [16], P('band'), may hold values from -0.5 to 0.5
Outputs:
- gradient: float32 [4, 8, 256, 256], P('band', 'facet')
All inputs are finite; a program needn't handle non-finite values.
Results may differ from a plain program's by a relative error of at most 0.0003.
Values sent between devices are 32-bit elements; how exact they have to be, the bound alone decides.
A program may use at most 64 MiB of HBM per device.

v0:
```python
import numpy as np
import jax
import jax.numpy as jnp
from jax import lax
from jax.sharding import PartitionSpec as P

B = 64
TERMS = 4
FGY = 4
HIGH = lax.Precision.HIGH


def padded(array, sides, width):
    for axis, dim in sides:
        peers, length = (lax.axis_size(axis), array.shape[dim])
        up = [(i, (i + 1) % peers) for i in range(peers)]
        down = [(j, i) for i, j in up]
        last = lax.slice_in_dim(array, length - width, length, axis=dim)
        initial = lax.slice_in_dim(array, 0, width, axis=dim)
        before = lax.ppermute(last, axis, up)
        after = lax.ppermute(initial, axis, down)
        array = jnp.concatenate([before, array, after], axis=dim)
    return array


def shifted(array, axis, by):
    peers = lax.axis_size(axis)
    return lax.ppermute(array, axis, [(i, (i + by) % peers) for i in range(peers)])


def extend(field, column, row_of):
    inner = field.shape[1]
    wide = padded(field, (("facet", 2),), B)
    positions = jnp.arange(inner + 2 * B)
    keep_left = column > 0
    keep_right = column < FGY - 1
    keep = jnp.where(positions < B, keep_left, jnp.where(positions >= B + inner, keep_right, True))
    wide = jnp.where(keep[None, None, :], wide, 0.0)
    above = shifted(wide[:, inner - B :, :], "facet", FGY)
    below = shifted(wide[:, :B, :], "facet", -FGY)
    above = jnp.where(row_of > 0, above, 0.0)
    below = jnp.where(row_of < lax.axis_size("facet") // FGY - 1, below, 0.0)
    return jnp.concatenate([above, wide, below], axis=1)


def forward_table(positions, length, half):
    k = np.arange(half)
    angle = 2 * np.pi * ((k[:, None] * positions[None, :]) % length) / length
    ok = (k <= length // 2)[:, None]
    return np.concatenate([np.cos(angle) * ok, np.sin(angle) * ok], axis=0)


def inverse_table(positions, length, half):
    k = np.arange(half)
    fold = np.where((k == 0) | (k == length // 2), 1.0, 2.0) / length
    return forward_table(positions, length, half) * np.concatenate([fold, fold])[:, None]


def powers(band_offset, count):
    columns = [jnp.ones_like(band_offset)]
    for _ in range(1, count):
        columns.append(columns[-1] * band_offset)
    return jnp.stack(columns, axis=1)


def dot(a, b):
    return jnp.matmul(a, b, precision=HIGH)


def halves(x, hr, hc):
    cc, cs = x[..., :hr, :hc], x[..., :hr, hc:]
    sc, ss = x[..., hr:, :hc], x[..., hr:, hc:]
    return (cc - ss, sc + cs, cc + ss, sc - cs)


def body(coeffs, dirty, psf, band_offset):
    size = coeffs.shape[-1]
    span = size + 2 * B
    k = psf.shape[-1]
    hr, hc = 200, 256
    pos = np.arange(span) - B
    ker = np.arange(k) - B
    out = np.arange(size)
    f32 = lambda a: jnp.asarray(a.astype(np.float32))
    ar, ac = f32(forward_table(pos, span, hr)), f32(forward_table(pos, span, hc).T)
    pr, pc = f32(forward_table(ker, span, hr)), f32(forward_table(ker, span, hc).T)
    br, bc = f32(inverse_table(out, span, hr).T / 2), f32(inverse_table(out, span, hc))

    facets = lax.axis_size("facet")
    position = (lax.axis_index("facet") + FGY + FGY // 2) % facets
    window = extend(coeffs[:, 0], position % FGY, position // FGY)[0]
    weights = powers(band_offset, 2 * TERMS - 1)
    combos = jnp.einsum("bs,bij->sij", weights, psf[:, 0], precision=HIGH)
    combos = lax.psum(combos, "band")
    mine = lax.dynamic_slice_in_dim(combos, lax.axis_index("band"), TERMS, axis=0)
    field = dot(ar, dot(window, ac))
    kern = dot(pr, dot(mine, pc))
    a, b, c, d = halves(field, hr, hc)
    e, f, g, h = halves(kern, hr, hc)
    re1, im1 = a * e - b * f, a * f + b * e
    re2, im2 = c * g - d * h, c * h + d * g
    z = jnp.concatenate(
        [
            jnp.concatenate([re1 + re2, im1 - im2], axis=2),
            jnp.concatenate([im1 + im2, re2 - re1], axis=2),
        ],
        axis=1,
    )
    smeared = dot(dot(br, z), bc)
    partial = jnp.einsum("bt,bij->tij", weights[:, :TERMS], dirty[:, 0], precision=HIGH) - smeared
    share = lax.psum_scatter(partial, "band", scatter_dimension=0, tiled=True)
    return share[:, None]


def solution(mesh):
    placed = (
        P("band", "facet", None, None),
        P("band", "facet", None, None),
        P("band", "facet", None, None),
        P("band"),
    )
    return jax.shard_map(
        body, mesh=mesh, in_specs=placed, out_specs=P("band", "facet", None, None), check_vma=False
    )
```

profile of v0, /device:TPU:0, one launch (start us, length us, event | category | flops | bytes accessed | tf_op | source)
XLA Modules:
  0.0 97.2 jit_solution(3402448764266653567)
XLA Ops:
  6.5 1.2 %fusion.43 = (f32[1,256,64]{2,1,0:T(8,128)S(1)}, f32[1,256,64]{2,1,0:T(8,128)S(1)}) fusion(f32[1,256,256]{2,1,0:T(8,128)} %bitcast.46), kind=kLoop, calls=%fused_computation.66 | loop fusion | bytes 262144 | tf_op jit(solution)/shard_map/slice | solution.py:18
  7.7 3.0 %collective-permute-start = (f32[1,256,64]{2,1,0:T(8,128)S(1)}, f32[1,256,64]{2,1,0:T(8,128)S(1)}, u32[]{:S(2)}, u32[]{:S(2)}) collective-permute-start(f32[1,256,64]{2,1,0:T(8,128)S(1)} %get-tuple-element.20), channel_id=1, source_target_pairs={{0,1},{1,2},{2,3},{3,4},{4,5},{5,6},{6,7},{7,0},{8,9},{9,10},{10,1... | collective-permute-start | bytes 196616 | tf_op jit(solution)/shard_map/ppermute | solution.py:20
  10.7 3.1 %collective-permute-start.1 = (f32[1,256,64]{2,1,0:T(8,128)S(1)}, f32[1,256,64]{2,1,0:T(8,128)S(1)}, u32[]{:S(2)}, u32[]{:S(2)}) collective-permute-start(f32[1,256,64]{2,1,0:T(8,128)S(1)} %get-tuple-element.21), channel_id=1, source_target_pairs={{1,0},{2,1},{3,2},{4,3},{5,4},{6,5},{7,6},{0,7},{9,8},{10,9},{11,1... | collective-permute-start | bytes 196616 | tf_op jit(solution)/shard_map/ppermute | solution.py:21
  13.8 0.7 multiply_bitcast_fusion.1
  14.5 0.7 stack.30
  15.2 2.6 %fusion.22 = f32[7,129,129]{2,0,1:T(8,128)} fusion(f32[4,1,129,129]{3,1,2,0:T(1,128)} %param.12, f32[4,7]{0,1:T(8,128)S(1)} %stack.30), kind=kOutput, calls=%fused_computation.30 | convolution fusion | flops 2795688 | bytes 732316 | tf_op jit(solution)/shard_map/bs,bij->sij/dot_general | solution.py:93
  18.0 0.6 collective-permute-done.1
  18.7 0.7 fusion.42
  19.4 2.2 %collective-permute-start.2 = (f32[1,64,384]{2,1,0:T(8,128)}, f32[1,64,384]{2,1,0:T(8,128)S(1)}, u32[]{:S(2)}, u32[]{:S(2)}) collective-permute-start(f32[1,64,384]{2,1,0:T(8,128)} %get-tuple-element.18), channel_id=1, source_target_pairs={{0,4},{1,5},{2,6},{3,7},{4,0},{5,1},{6,2},{7,3},{8,12},{9,13},{10,... | collective-permute-start | bytes 294920 | tf_op jit(solution)/shard_map/ppermute | solution.py:28
  21.6 1.6 %fusion.13 = f32[4,256,256]{2,0,1:T(4,128)S(1)} fusion(f32[4,256,256]{2,1,0:T(8,128)S(1)} %bitcast.45, f32[4,1]{0,1:T(1,128)S(1)} %get-tuple-element.24, f32[4,1]{0,1:T(1,128)S(1)} %get-tuple-element.25, f32[4,1]{0,1:T(1,128)S(1)} %bitcast.49, f32[4,1]{0,1:T(1,128)S(1)} %broadcast.62), kind=kOutput, calls=%fused_computation.12 | convolution fusion | flops 6291504 | bytes 2097216 | tf_op jit(solution)/shard_map/bt,bij->tij/dot_general | solution.py:110
  23.2 0.8 collective-permute-start.3
  24.0 3.2 %collective-permute-done.2 = f32[1,64,384]{2,1,0:T(8,128)S(1)} collective-permute-done((f32[1,64,384]{2,1,0:T(8,128)}, f32[1,64,384]{2,1,0:T(8,128)S(1)}, u32[]{:S(2)}, u32[]{:S(2)}) %collective-permute-start.2) | collective-permute-done | bytes 98336 | tf_op jit(solution)/shard_map/ppermute | solution.py:28
  27.3 3.9 %collective-permute-done.3 = f32[1,64,384]{2,1,0:T(8,128)S(1)} collective-permute-done((f32[1,64,384]{2,1,0:T(8,128)S(1)}, f32[1,64,384]{2,1,0:T(8,128)S(1)}, u32[]{:S(2)}, u32[]{:S(2)}) %collective-permute-start.3) | collective-permute-done | bytes 98336 | tf_op jit(solution)/shard_map/ppermute | solution.py:28
  31.2 0.8 fusion.15
  32.0 0.8 fusion.44
  32.9 20.0 %all-reduce.2.cloned.1.call-done = f32[7,129,129]{2,0,1:T(8,128)} async-done(((f32[7,129,129]{2,0,1:T(8,128)}), f32[7,129,129]{2,0,1:T(8,128)}) %all-reduce.2.cloned.1.call-update) | async-done | bytes 465964 | tf_op jit(solution)/shard_map/psum | solution.py:94
  52.9 1.3 %constant_dynamic-slice_fusion = f32[4,129,129]{2,0,1:T(4,128)S(1)} fusion(f32[7,129,129]{2,0,1:T(8,128)} %all-reduce.2.cloned.1.call-done, s32[]{:T(128)S(6)} %select_n.70), kind=kLoop, calls=%fused_computation.58 | loop fusion | bytes 532516 | tf_op jit(solution)/shard_map/dynamic_slice | solution.py:95
  54.2 0.6 fusion.20
  54.8 1.9 %convolution_bitcast_fusion = f32[4,400,512]{2,1,0:T(8,128)S(1)} fusion(f32[4,129,512]{2,1,0:T(8,128)S(1)} %fusion.20, f32[400,129,1]{0,1,2:T(8,128)S(1)} %copy-done.5), kind=kOutput, calls=%fused_computation.10 | convolution fusion | flops 634060800 | bytes 4539968 | tf_op jit(solution)/shard_map/dot_general | solution.py:67
  56.7 0.6 fusion.41
  57.5 0.8 copy-done.8
  58.3 3.6 %fusion = f32[4,512,256]{2,1,0:T(8,128)S(1)} fusion(f32[256,400,1]{0,1,2:T(8,128)S(1)} %copy-done.8, f32[4,200,256]{2,1,0:T(8,128)S(1)} %sub.39, f32[4,200,256]{2,1,0:T(8,128)S(1)} %add.56, f32[4,200,256]{2,1,0:T(8,128)S(1)} %get-tuple-element.8, f32[4,200,256]{2,1,0:T(8,128)S(1)} %get-tuple-element.11), kind=kOutput, calls=%fused_computation | convolution fusion | flops 1260748800 | bytes 5783552 | tf_op jit(solution)/shard_map/dot_general | solution.py:67
  61.9 2.9 %fusion.10 = f32[4,256,256]{2,1,0:T(8,128)} fusion(f32[512,256,1]{1,0,2:T(8,128)S(1)} %copy-done.4, f32[4,512,256]{2,1,0:T(8,128)S(1)} %fusion, f32[4,256,256]{2,0,1:T(4,128)S(1)} %fusion.13), kind=kOutput, calls=%fused_computation.11 | convolution fusion | flops 805568512 | bytes 4718592 | tf_op jit(solution)/shard_map/dot_general | solution.py:67
  64.8 25.6 %reduce-scatter.2.cloned.1.call-done = f32[1,256,256]{2,1,0:T(8,128)} async-done(((f32[4,256,256]{2,1,0:T(8,128)}), f32[1,256,256]{2,1,0:T(8,128)}) %reduce-scatter.2.cloned.1.call-update) | async-done | bytes 262160 | tf_op jit(solution)/shard_map/reduce_scatter | solution.py:111
  (30 shorter events, 0.6 us)
Async XLA Ops:
  6.5 15.1 %copy-start = (f32[4,1,256,256]{3,2,1,0:T(8,128)S(1)}, f32[4,1,256,256]{3,2,1,0:T(8,128)}, u32[]{:S(2)}) copy-start(f32[4,1,256,256]{3,2,1,0:T(8,128)} %param.11) | copy-start | bytes 3145732
  6.5 12.0 %copy-start.1 = (f32[1,1,256,256]{3,2,1,0:T(8,128)S(1)}, f32[1,1,256,256]{3,2,1,0:T(8,128)}, u32[]{:S(2)}) copy-start(f32[1,1,256,256]{3,2,1,0:T(8,128)} %param.10) | copy-start | bytes 786436
  6.5 46.3 %all-reduce.2.cloned.1.call-start = ((), (), s32[]{:S(2)}) async-start(), calls=%async_computation.1 | async-start | bytes 2113536 | tf_op jit(solution)/shard_map/psum | solution.py:94
  7.7 13.9 %copy-start.7 = (f32[4]{0:T(128)S(1)}, f32[4]{0:T(128)}, u32[]{:S(2)}) copy-start(f32[4]{0:T(128)} %param.13) | copy-start | bytes 52
  7.7 10.2 %collective-permute-start = (f32[1,256,64]{2,1,0:T(8,128)S(1)}, f32[1,256,64]{2,1,0:T(8,128)S(1)}, u32[]{:S(2)}, u32[]{:S(2)}) collective-permute-start(f32[1,256,64]{2,1,0:T(8,128)S(1)} %get-tuple-element.20), channel_id=1, source_target_pairs={{0,1},{1,2},{2,3},{3,4},{4,5},{5,6},{6,7},{7,0},{8,9},{9,10},{10,1... | collective-permute-start | bytes 196616 | tf_op jit(solution)/shard_map/ppermute | solution.py:20
  10.7 7.8 %collective-permute-start.1 = (f32[1,256,64]{2,1,0:T(8,128)S(1)}, f32[1,256,64]{2,1,0:T(8,128)S(1)}, u32[]{:S(2)}, u32[]{:S(2)}) collective-permute-start(f32[1,256,64]{2,1,0:T(8,128)S(1)} %get-tuple-element.21), channel_id=1, source_target_pairs={{1,0},{2,1},{3,2},{4,3},{5,4},{6,5},{7,6},{0,7},{9,8},{10,9},{11,1... | collective-permute-start | bytes 196616 | tf_op jit(solution)/shard_map/ppermute | solution.py:21
  17.8 13.3 %copy-start.2 = (f32[384,512]{1,0:T(8,128)S(1)}, f32[384,512]{1,0:T(8,128)}, u32[]{:S(2)}) copy-start(f32[384,512]{1,0:T(8,128)} %constant.74.clone) | copy-start | bytes 2359300
  17.9 72.5 %reduce-scatter.2.cloned.1.call-start = ((), (), s32[]{:S(2)}) async-start(), calls=%async_computation.2 | async-start | bytes 1310720 | tf_op jit(solution)/shard_map/reduce_scatter | solution.py:111
  19.4 7.9 %collective-permute-start.2 = (f32[1,64,384]{2,1,0:T(8,128)}, f32[1,64,384]{2,1,0:T(8,128)S(1)}, u32[]{:S(2)}, u32[]{:S(2)}) collective-permute-start(f32[1,64,384]{2,1,0:T(8,128)} %get-tuple-element.18), channel_id=1, source_target_pairs={{0,4},{1,5},{2,6},{3,7},{4,0},{5,1},{6,2},{7,3},{8,12},{9,13},{10,... | collective-permute-start | bytes 294920 | tf_op jit(solution)/shard_map/ppermute | solution.py:28
  23.2 8.7 %copy-start.3 = (f32[400,384]{1,0:T(8,128)S(1)}, f32[400,384]{1,0:T(8,128)}, u32[]{:S(2)}) copy-start(f32[400,384]{1,0:T(8,128)} %constant.73.clone) | copy-start | bytes 1843204
  23.2 7.9 %collective-permute-start.3 = (f32[1,64,384]{2,1,0:T(8,128)S(1)}, f32[1,64,384]{2,1,0:T(8,128)S(1)}, u32[]{:S(2)}, u32[]{:S(2)}) collective-permute-start(f32[1,64,384]{2,1,0:T(8,128)S(1)} %get-tuple-element.19), channel_id=1, source_target_pairs={{0,4},{1,5},{2,6},{3,7},{4,0},{5,1},{6,2},{7,3},{8,12},{9,13},{10,... | collective-permute-start | bytes 294920 | tf_op jit(solution)/shard_map/ppermute | solution.py:28
  32.0 22.2 %copy-start.6 = (f32[129,512,1]{1,0,2:T(8,128)S(1)}, f32[129,512,1]{1,0,2:T(8,128)}, u32[]{:S(2)}) copy-start(f32[129,512,1]{1,0,2:T(8,128)} %constant.82) | copy-start | bytes 792580
  32.8 22.0 %copy-start.5 = (f32[400,129,1]{0,1,2:T(8,128)S(1)}, f32[400,129,1]{0,1,2:T(8,128)}, u32[]{:S(2)}) copy-start(f32[400,129,1]{0,1,2:T(8,128)} %constant.83) | copy-start | bytes 619204
  57.3 1.0 %copy-start.8 = (f32[256,400,1]{0,1,2:T(8,128)S(1)}, f32[256,400,1]{0,1,2:T(8,128)}, u32[]{:S(2)}) copy-start(f32[256,400,1]{0,1,2:T(8,128)} %constant.84) | copy-start | bytes 1228804
  58.3 3.6 %copy-start.4 = (f32[512,256,1]{1,0,2:T(8,128)S(1)}, f32[512,256,1]{1,0,2:T(8,128)}, u32[]{:S(2)}) copy-start(f32[512,256,1]{1,0,2:T(8,128)} %constant.85) | copy-start | bytes 1572868
Sparse Core Ops, SparseCore 0:
  18.0 34.8 all-reduce.1
  65.0 25.3 reduce-scatter.1
where the time goes:
time: 97.5 us; the launch traced here: 97.2 us
  waiting for transfers between devices  53.2 us (55%)
  matrix products  14.8 us (15%)
  between operations  13.7 us (14%)
  starting transfers between devices  9.16 us (9%)
  local copies, waits for them, and re-layouts  4.65 us (5%)
  other arithmetic  1.74 us (2%)
    reduce_scatter x1, waiting for transfers between devices, body(): share = lax.psum_scatter(partial, 'band', scatter_dimension=0, tiled=True)  25.6 us
    psum x1, waiting for transfers between devices, body(): combos = lax.psum(combos, 'band')  20 us
    dot_general x6, matrix products, dot(): return jnp.matmul(a, b, precision=HIGH)  10.6 us
    ppermute x2, waiting for transfers between devices, shifted(): lax.ppermute(array, axis, [(i, (i + by) % peers) for i in range(peers)])  7.13 us
    ppermute x1, starting transfers between devices, padded(): after = lax.ppermute(initial, axis, down)  3.1 us
    ppermute x1, starting transfers between devices, padded(): before = lax.ppermute(last, axis, up)  3.02 us
    ppermute x2, starting transfers between devices, shifted(): lax.ppermute(array, axis, [(i, (i + by) % peers) for i in range(peers)])  2.99 us
    dot_general x1, matrix products, body(): combos = jnp.einsum('bs,bij->sij', weights, psf[:, 0], precision=HIGH)  2.63 us
  transfers between devices with their start and end apart: 6, of which 5 were waited for; matrix products, arithmetic and copies ran while one was open for 8% of the time, Pallas kernels for 0%

commit v1 on v0

v1 whole, which is shorter than its diff:
```python
import ml_dtypes
import numpy as np
import jax
import jax.numpy as jnp
from jax import lax
from jax.experimental import pallas as pl
from jax.experimental.pallas import tpu as pltpu
from jax.sharding import PartitionSpec as P

B = 64
TERMS = 4
FGY = 4
POWERS = 2 * TERMS - 1
HR = 208
HC = 256
KROWS = 144
LANES = 128
F32 = jnp.float32
BF16 = jnp.bfloat16
NEIGHBOURS = [(dr, dc) for dr in (-1, 0, 1) for dc in (-1, 0, 1) if (dr, dc) != (0, 0)]


def forward_table(positions, length, half):
    k = np.arange(half)
    angle = 2 * np.pi * ((k[:, None] * positions[None, :]) % length) / length
    ok = (k <= length // 2)[:, None]
    return np.concatenate([np.cos(angle) * ok, np.sin(angle) * ok], axis=0)


def inverse_table(positions, length, half):
    k = np.arange(half)
    fold = np.where((k == 0) | (k == length // 2), 1.0, 2.0) / length
    return forward_table(positions, length, half) * np.concatenate([fold, fold])[:, None]


def split_table(table):
    hi = table.astype(np.float32).astype(ml_dtypes.bfloat16)
    lo = (table - hi.astype(np.float64)).astype(np.float32).astype(ml_dtypes.bfloat16)
    return hi, lo


def left_table(table, width):
    hi, lo = split_table(table)
    whole = np.concatenate([hi, hi, lo], axis=1)
    return np.pad(whole, ((0, 0), (0, width - whole.shape[1])))


def right_table(table):
    hi, lo = split_table(table)
    return np.concatenate([hi, lo, hi], axis=0)


def tables(size, span, k):
    pos = np.arange(span)
    out = np.arange(size)
    ker = np.arange(k) - B
    field_cols = right_table(forward_table(pos, span, HC).T)
    field_rows = left_table(forward_table(pos, span, HR), 3 * span)
    kern = forward_table(ker, span, HC).T
    kern = np.concatenate([kern[:LANES], np.repeat(kern[LANES:], LANES, axis=0)], axis=0)
    kern_cols = right_table(kern)
    rows = np.pad(forward_table(ker, span, HR), ((0, 0), (0, KROWS - k)))
    kern_rows = left_table(rows, 512)
    back_rows = left_table(inverse_table(out, span, HR).T / 2, 1280)
    back_cols = right_table(inverse_table(out, span, HC))
    return field_cols, field_rows, kern_cols, kern_rows, back_rows, back_cols


def split(x):
    hi = x.astype(BF16)
    return hi, (x - hi.astype(F32)).astype(BF16)


def put_left(ref, x, rows):
    hi, lo = split(x)
    w = x.shape[1]
    ref[rows, 0:w] = hi
    ref[rows, w : 2 * w] = hi
    ref[rows, 2 * w : 3 * w] = lo


def put_right(ref, x, at=0, pitch=None):
    hi, lo = split(x)
    h = x.shape[0]
    pitch = pitch or h
    ref[at : at + h] = hi
    ref[pitch + at : pitch + at + h] = lo
    ref[2 * pitch + at : 2 * pitch + at + h] = hi


def dot(a, b):
    return jnp.dot(a, b, preferred_element_type=F32)


def half_mask(shape):
    return lax.broadcasted_iota(jnp.int32, shape, 1) < LANES // 2


def pack(first, second, left):
    mask = half_mask(first.shape)
    moved = pltpu.roll(second, LANES // 2, 1)
    return jnp.where(mask, first, moved) if left else jnp.where(mask, moved, first)


def kernel(
    facets, size, bands,
    coeffs, dirty_hbm, psf, offset, *refs,
):
    tables_hbm = refs[:6]
    out = refs[6]
    (fc, fr, kc, kr, br, bc, dirty, local_sem,
     comb, recv_a, recv_b, fsum, xrecv, side, side_in, corner, corner_in, vert_in,
     xl, yr, pleft, kright, zright, wleft, field, kern, part, pair_in, term_x, term_in,
     halo_send, halo_recv, s_send, s_recv, x_send, x_recv, f_send, f_recv,
     t_send, t_recv) = refs[7:]
    span = size + 2 * B
    vm = (fc, fr, kc, kr, br, bc)

    g = lax.axis_index("band")
    facet = lax.axis_index("facet")
    chip, core = g // 2, g % 2
    sib = {"band": 2 * chip + 1 - core}
    far = {"band": 2 * (1 - chip) + core}
    q = (facet + FGY + FGY // 2) % facets
    row, col = q // FGY, q % FGY

    local = [pltpu.make_async_copy(tables_hbm[i], vm[i], local_sem.at[i]) for i in range(6)]
    local.append(pltpu.make_async_copy(dirty_hbm, dirty, local_sem.at[6]))
    for copy in local:
        copy.start()

    def exists(d):
        r, c = row + d[0], col + d[1]
        return (r >= 0) & (r < facets // FGY) & (c >= 0) & (c < FGY)

    def device(d):
        return {"facet": (facet + FGY * d[0] + d[1] + facets) % facets}

    barrier = pltpu.get_barrier_semaphore()
    count = 2
    for d in NEIGHBOURS:
        there = exists(d)
        count = count + there.astype(jnp.int32)

        @pl.when(there)
        def _():
            pl.semaphore_signal(barrier, inc=1, device_id=device(d))

    for peer in (sib, far):
        pl.semaphore_signal(barrier, inc=1, device_id=peer)

    powers = []
    for b in range(bands):
        w = offset[b]
        row_b = [jnp.float32(1.0)]
        for _ in range(1, POWERS):
            row_b.append(row_b[-1] * w)
        powers.append(row_b)

    k = psf.shape[-1]
    late = chip == 1

    def place(s):
        return s + jnp.where(late & (s >= 5), 1, 0)

    last = jnp.where(late, 5, 7)
    lane = lax.broadcasted_iota(jnp.int32, (1, LANES), 1)
    comb[:, LANES:KROWS, :] = jnp.zeros((8, KROWS - LANES, LANES), F32)
    for s in range(POWERS):
        total = psf[0, 0, :, 0:LANES]
        if s:
            total = total * powers[0][s]
        for b in range(1, bands):
            total += psf[b, 0, :, 0:LANES] * powers[b][s]
        comb[place(jnp.int32(s)), 0:k, :] = total
    total = jnp.zeros((k, LANES), F32)
    for b in range(bands):
        w_row = jnp.zeros((1, LANES), F32)
        for s in range(POWERS):
            w_row = jnp.where(lane == s, powers[b][s], w_row)
        total += psf[b, 0, :, LANES:k] * w_row
    comb[last, 0:k, :] = total

    h = size // 2
    side[0] = pack(coeffs[0, 0, 0:h, 0:LANES], coeffs[0, 0, h:size, 0:LANES], True)
    side[1] = pack(
        coeffs[0, 0, 0:h, size - LANES : size], coeffs[0, 0, h:size, size - LANES : size], False
    )
    for i, top in enumerate((0, size - B)):
        for j in range(2):
            lanes = slice(0, LANES) if j == 0 else slice(size - LANES, size)
            corner[2 * i + j] = pack(
                coeffs[0, 0, top : top + B // 2, lanes],
                coeffs[0, 0, top + B // 2 : top + B, lanes],
                j == 0,
            )

    def halo(d):
        dr, dc = d
        if dr == 0:
            i = (dc + 1) // 2
            src, dst = side.at[i], side_in.at[i]
        elif dc == 0:
            i = (dr + 1) // 2
            src = coeffs.at[0, 0, pl.ds(i * (size - B), B), :]
            dst = vert_in.at[i]
        else:
            i = (dr + 1) + (dc + 1) // 2
            src, dst = corner.at[i], corner_in.at[i]
        n = NEIGHBOURS.index(d)
        return pltpu.make_async_remote_copy(
            src, dst, halo_send.at[n], halo_recv.at[n], device_id=device(d)
        )

    pl.semaphore_wait(barrier, count)

    def start_of(c, who):
        return 2 * (1 - who) + 3 * c

    a_copy = pltpu.make_async_remote_copy(
        comb.at[pl.ds(start_of(1 - core, chip), 3)], recv_a, s_send.at[0], s_recv.at[0], device_id=sib
    )
    a_copy.start()
    order = sorted(NEIGHBOURS, key=lambda d: abs(d[0]) + abs(d[1]) == 2)
    for d in order:
        @pl.when(exists(d))
        def _():
            halo(d).start()

    b_copy = pltpu.make_async_remote_copy(comb, recv_b, s_send.at[1], s_recv.at[1], device_id=sib)
    b_copy.start()

    a_copy.wait_recv()
    mine = start_of(core, chip)
    x_copies, f_copies = [], []
    for i in range(3):
        fsum[i] = comb[mine + i] + recv_a[i]
        slot = xrecv.at[3 * core + i]
        x_copies.append(
            pltpu.make_async_remote_copy(fsum.at[i], slot, x_send.at[i], x_recv.at[i], device_id=far)
        )
        f_copies.append(
            pltpu.make_async_remote_copy(slot, slot, f_send.at[i], f_recv.at[i], device_id=sib)
        )
        x_copies[i].start()

    for d in NEIGHBOURS:
        dr, dc = d
        there = exists(d)
        incoming = halo((-dr, -dc))

        @pl.when(there)
        def _():
            incoming.wait_recv()

        if dr == 0:
            ref, i = side_in, (1 - dc) // 2
        elif dc == 0:
            ref, i = vert_in, (1 - dr) // 2
        else:
            ref, i = corner_in, (1 - dr) + (1 - dc) // 2

        @pl.when(jnp.logical_not(there))
        def _():
            ref[i] = jnp.zeros(ref.shape[1:], F32)

    for i in range(3):
        x_copies[i].wait_recv()
        f_copies[i].start()

    mask = half_mask((h, LANES))
    small = half_mask((B // 2, LANES))
    local[0].wait()

    def edge(right, left, m):
        top = jnp.where(m, right, left)
        bottom = pltpu.roll(jnp.where(m, left, right), LANES // 2, 1)
        return top, bottom

    def window(rows, centre, strip):
        put_left(xl, jnp.concatenate([centre, strip], axis=1), rows)

    top, bottom = edge(side_in[0], side_in[1], mask)
    window(pl.ds(0, h), coeffs[0, 0, 0:h, :], top)
    window(pl.ds(h, h), coeffs[0, 0, h:size, :], bottom)
    for i in range(2):
        top, bottom = edge(corner_in[2 * i], corner_in[2 * i + 1], small)
        at = size + i * B
        window(pl.ds(at, B), vert_in[i], jnp.concatenate([top, bottom], axis=0))
    put_right(yr, dot(xl[...], fc[...]))
    local[1].wait()
    full = dot(fr[...], yr[...])

    def halves(x, ref):
        cc, cs = x[:HR, :HC], x[:HR, HC:]
        sc, ss = x[HR:, :HC], x[HR:, HC:]
        ref[0] = cc - ss
        ref[1] = sc + cs
        ref[2] = cc + ss
        ref[3] = sc - cs

    halves(full, field)

    for i in range(3):
        other = xrecv.at[3 * (1 - core) + i]
        pltpu.make_async_remote_copy(
            other, other, f_send.at[i], f_recv.at[i], device_id=sib
        ).wait_recv()
    b_copy.wait_recv()
    local[2].wait()
    local[3].wait()
    kright[3 * KROWS : 512] = jnp.zeros((512 - 3 * KROWS, 2 * HC), BF16)
    zright[6 * HR : 1280] = jnp.zeros((1280 - 6 * HR, 2 * HC), BF16)
    column = comb[last] + recv_b[last] + xrecv[5]

    @pl.loop(0, TERMS)
    def _(t):
        s = g + t
        at = place(s)
        main = comb[at] + recv_b[at] + xrecv[core + t]
        own = jnp.where(lane == s, column, 0.0)
        put_left(pleft, jnp.concatenate([main, own], axis=1), slice(0, KROWS))
        put_right(kright, dot(pleft[...], kc[...]))
        halves(dot(kr[...], kright[...]), kern.at[t])

    for copy in local[4:]:
        copy.wait()

    def weight(b, t):
        w = powers[b]
        return jnp.where(t == 0, w[0], jnp.where(t == 1, w[1], jnp.where(t == 2, w[2], w[3])))

    def term(t):
        a, b, c, d = (field[i] for i in range(4))
        e, f, p, r = (kern[t, i] for i in range(4))
        re1, im1 = a * e - b * f, a * f + b * e
        re2, im2 = c * p - d * r, c * r + d * p
        put_right(zright, jnp.concatenate([re1 + re2, im1 - im2], axis=1), 0, 2 * HR)
        put_right(zright, jnp.concatenate([im1 + im2, re2 - re1], axis=1), HR, 2 * HR)
        put_left(wleft, dot(br[...], zright[...]), slice(0, size))
        total = dirty[0, 0] * weight(0, t)
        for n in range(1, bands):
            total += dirty[n, 0] * weight(n, t)
        return total - dot(wleft[...], bc[...])

    def pair_copy(i):
        return pltpu.make_async_remote_copy(
            part.at[i], pair_in.at[i], t_send.at[i], t_recv.at[i], device_id=sib
        )

    away, home = 2 * (1 - chip), 2 * chip
    part[0] = term(away + 1 - core)
    first = pair_copy(0)
    first.start()
    total = term(away + core)
    first.wait_recv()
    term_x[...] = total + pair_in[0]
    cross = pltpu.make_async_remote_copy(
        term_x, term_in, t_send.at[2], t_recv.at[2], device_id=far
    )
    cross.start()
    part[1] = term(home + 1 - core)
    second = pair_copy(1)
    second.start()
    total = term(home + core)
    second.wait_recv()
    total += pair_in[1]
    cross.wait_recv()
    out[0, 0] = total + term_in[...]

    for d in NEIGHBOURS:
        @pl.when(exists(d))
        def _():
            halo(d).wait_send()

    for copy in (a_copy, b_copy, *x_copies, *f_copies, first, second, cross):
        copy.wait_send()


def body(coeffs, dirty, psf, band_offset):
    size = coeffs.shape[-1]
    span = size + 2 * B
    bands = dirty.shape[0]
    facets = lax.axis_size("facet")
    consts = tables(size, span, psf.shape[-1])
    vmem = pl.BlockSpec(memory_space=pltpu.VMEM)
    hbm = pl.BlockSpec(memory_space=pl.ANY)
    dma = lambda n: pltpu.SemaphoreType.DMA((n,))
    scratch = [pltpu.VMEM(c.shape, BF16) for c in consts]
    scratch += [
        pltpu.VMEM(dirty.shape, F32),
        dma(7),
        pltpu.VMEM((8, KROWS, LANES), F32),
        pltpu.VMEM((3, KROWS, LANES), F32),
        pltpu.VMEM((8, KROWS, LANES), F32),
        pltpu.VMEM((3, KROWS, LANES), F32),
        pltpu.VMEM((6, KROWS, LANES), F32),
        pltpu.VMEM((2, size // 2, LANES), F32),
        pltpu.VMEM((2, size // 2, LANES), F32),
        pltpu.VMEM((4, B // 2, LANES), F32),
        pltpu.VMEM((4, B // 2, LANES), F32),
        pltpu.VMEM((2, B, size), F32),
        pltpu.VMEM((span, 3 * span), BF16),
        pltpu.VMEM((3 * span, 2 * HC), BF16),
        pltpu.VMEM((KROWS, 6 * LANES), BF16),
        pltpu.VMEM((512, 2 * HC), BF16),
        pltpu.VMEM((1280, 2 * HC), BF16),
        pltpu.VMEM((size, 6 * HC), BF16),
        pltpu.VMEM((4, HR, HC), F32),
        pltpu.VMEM((TERMS, 4, HR, HC), F32),
        pltpu.VMEM((2, size, size), F32),
        pltpu.VMEM((2, size, size), F32),
        pltpu.VMEM((size, size), F32),
        pltpu.VMEM((size, size), F32),
        dma(8), dma(8), dma(2), dma(2), dma(3), dma(3), dma(3), dma(3), dma(3), dma(3),
    ]

    def run(*args):
        kernel(facets, size, bands, *args)

    return pl.pallas_call(
        run,
        out_shape=jax.ShapeDtypeStruct(coeffs.shape, F32),
        in_specs=[vmem, hbm, vmem, pl.BlockSpec(memory_space=pltpu.SMEM)] + [hbm] * 6,
        out_specs=vmem,
        scratch_shapes=scratch,
        compiler_params=pltpu.CompilerParams(
            collective_id=0, has_side_effects=True, vmem_limit_bytes=56 * 1024 * 1024
        ),
        cost_estimate=pl.CostEstimate(flops=4_000_000_000, bytes_accessed=8_000_000, transcendentals=0),
    )(coeffs, dirty, psf, band_offset, *[jnp.asarray(c) for c in consts])


def solution(mesh):
    placed = (
        P("band", "facet", None, None),
        P("band", "facet", None, None),
        P("band", "facet", None, None),
        P("band"),
    )
    return jax.shard_map(
        body, mesh=mesh, in_specs=placed, out_specs=P("band", "facet", None, None), check_vma=False
    )
```

time: 97.5 us -> 34.1 us (0.35)
  waiting for transfers between devices: 53.2 us -> 0 us
  Pallas kernels: 0 us -> 30.3 us
  matrix products: 14.8 us -> 0 us
  between operations: 13.7 us -> 0.01 us
  starting transfers between devices: 9.16 us -> 0 us
  other arithmetic: 1.74 us -> 0 us
  local copies, waits for them, and re-layouts: 4.65 us -> 3.55 us
    pallas_call x0 -> x1, Pallas kernels: none -> 30.3 us  [body(): pl.pallas_call(run, out_shape=jax.ShapeDtypeStruct(coeffs.shape, F32), in...]
    reduce_scatter x1 -> x0, waiting for transfers between devices: 25.6 us -> none  [body(): share = lax.psum_scatter(partial, 'band', scatter_dimension=0, tiled=True)]
    psum x1 -> x0, waiting for transfers between devices: 20 us -> none  [body(): combos = lax.psum(combos, 'band')]
    dot_general x8 -> x0, matrix products: 14.8 us -> none  [the longest x6 10.6 us: dot(): return jnp.matmul(a, b, precision=HIGH)]
    ppermute x4 -> x0, starting transfers between devices: 9.11 us -> none  [the longest x1 3.1 us: padded(): after = lax.ppermute(initial, axis, down)]
    ppermute x4 -> x0, waiting for transfers between devices: 7.69 us -> none  [the longest x2 7.13 us: shifted(): lax.ppermute(array, axis, [(i, (i + by) % peers) for i in range(peers)])]
    unnamed x18 -> x2, local copies, waits for them, and re-layouts: 0.81 us -> 3.55 us
    slice x2 -> x0, local copies, waits for them, and re-layouts: 1.81 us -> none  [the longest x1 1.16 us: padded(): last = lax.slice_in_dim(array, length - width, length, axis=dim)]
  transfers between devices with their start and end apart: 6 -> 0, of which waited for: 5 -> 0; matrix products, arithmetic and copies ran while one was open for 8% -> 0% of each run, Pallas kernels for 0% -> 0%
where the time goes in v1:
time: 34.1 us; the launch traced here: 33.9 us
  Pallas kernels  30.3 us (89%)
  local copies, waits for them, and re-layouts  3.55 us (10%)
    pallas_call x1, Pallas kernels, body(): pl.pallas_call(run, out_shape=jax.ShapeDtypeStruct(coeffs.shape, F32), in...  30.3 us
    unnamed x2, local copies, waits for them, and re-layouts  3.55 us

profile of v1, /device:TPU:0, one launch (start us, length us, event | category | flops | bytes accessed | tf_op | source)
XLA Modules:
  0.0 33.9 jit_solution(5033760703425420167)
XLA Ops:
  0.0 1.9 %copy.11.args_2_ = f32[4,1,129,129]{3,2,1,0:T(8,128)} copy(f32[4,1,129,129]{3,1,2,0:T(1,128)} %param.12) | data formatting | bytes 532512 | tf_op args[2]
  1.9 30.3 %shard_map.100 = f32[1,1,256,256]{3,2,1,0:T(8,128)} custom-call(f32[1,1,256,256]{3,2,1,0:T(8,128)} %args_0_.4, f32[4,1,256,256]{3,2,1,0:T(8,128)} %args_1_.4, f32[4,1,129,129]{3,2,1,0:T(8,128)} %copy.11.args_2_, f32[4]{0:T(128)} %args_3_.4, bf16[1152,512]{1,0:T(8,128)(2,1)} %constant.12.clone.args_4_, bf16[416,1152]{1,0:T(8,128)(2,1)} %constant.13.clone.args_5_, ...), custom_call_target="tpu_custom_call" | custom-call | flops 4000000000 | bytes 8000000 | tf_op jit(solution)/shard_map/pallas_call | solution.py:421
  32.2 1.7 %copy.13 = f32[1,1,256,256]{3,2,1,0:T(8,128)} copy(f32[1,1,256,256]{3,2,1,0:T(8,128)} %shard_map.100) | data formatting | bytes 524288

commit v2 on v1

v2 whole, which is shorter than its diff:
```python
import ml_dtypes
import numpy as np
import jax
import jax.numpy as jnp
from jax import lax
from jax.experimental import pallas as pl
from jax.experimental.pallas import tpu as pltpu
from jax.sharding import PartitionSpec as P

B = 64
TERMS = 4
FGY = 4
POWERS = 2 * TERMS - 1
ORDER = (2, 3, 4, None, 0, 1, 5, 6)
HR = 208
HC = 256
KROWS = 144
SENT = 136
LANES = 128
F32 = jnp.float32
BF16 = jnp.bfloat16
NEIGHBOURS = [(dr, dc) for dr in (-1, 0, 1) for dc in (-1, 0, 1) if (dr, dc) != (0, 0)]


def forward_table(positions, length, half):
    k = np.arange(half)
    angle = 2 * np.pi * ((k[:, None] * positions[None, :]) % length) / length
    ok = (k <= length // 2)[:, None]
    return np.concatenate([np.cos(angle) * ok, np.sin(angle) * ok], axis=0)


def inverse_table(positions, length, half):
    k = np.arange(half)
    fold = np.where((k == 0) | (k == length // 2), 1.0, 2.0) / length
    return forward_table(positions, length, half) * np.concatenate([fold, fold])[:, None]


def split_table(table):
    hi = table.astype(np.float32).astype(ml_dtypes.bfloat16)
    lo = (table - hi.astype(np.float64)).astype(np.float32).astype(ml_dtypes.bfloat16)
    return hi, lo


def left_table(table, width):
    hi, lo = split_table(table)
    whole = np.concatenate([hi, hi, lo], axis=1)
    return np.pad(whole, ((0, 0), (0, width - whole.shape[1])))


def right_table(table):
    hi, lo = split_table(table)
    return np.concatenate([hi, lo, hi], axis=0)


def tables(size, span, k):
    pos = np.arange(span)
    out = np.arange(size)
    ker = np.arange(k) - B
    cols = forward_table(pos, span, HC).T
    field_own, field_edge = right_table(cols[:size]), right_table(cols[size:])
    field_rows = left_table(forward_table(pos, span, HR), 3 * span)
    kern = forward_table(ker, span, HC).T
    kern = np.concatenate([kern[:LANES], np.repeat(kern[LANES:], LANES, axis=0)], axis=0)
    kern_cols = right_table(kern)
    rows = np.pad(forward_table(ker, span, HR), ((0, 0), (0, KROWS - k)))
    kern_rows = left_table(rows, 512)
    back_rows = left_table(inverse_table(out, span, HR).T / 2, 1280)
    back_cols = right_table(inverse_table(out, span, HC))
    return field_own, field_edge, field_rows, kern_cols, kern_rows, back_rows, back_cols


def split(x):
    hi = x.astype(BF16)
    return hi, (x - hi.astype(F32)).astype(BF16)


def put_left(ref, x, row=0):
    hi, lo = split(x)
    h, w = x.shape
    ref[row : row + h, 0:w] = hi
    ref[row : row + h, w : 2 * w] = hi
    ref[row : row + h, 2 * w : 3 * w] = lo


def put_right(ref, x, at=0, pitch=None):
    hi, lo = split(x)
    h = x.shape[0]
    pitch = pitch or h
    ref[at : at + h] = hi
    ref[pitch + at : pitch + at + h] = lo
    ref[2 * pitch + at : 2 * pitch + at + h] = hi


def dot(a, b):
    return jnp.dot(a, b, preferred_element_type=F32)


def half_mask(shape):
    return lax.broadcasted_iota(jnp.int32, shape, 1) < LANES // 2


def pack(first, second, left):
    mask = half_mask(first.shape)
    moved = pltpu.roll(second, LANES // 2, 1)
    return jnp.where(mask, first, moved) if left else jnp.where(mask, moved, first)


def kernel(
    facets, size, bands,
    coeffs, dirty_hbm, psf, offset, *refs,
):
    tables_hbm = refs[:7]
    out, got = refs[7:9]
    (fo, fe, fr, kc, kr, br, bc, dirty, local_sem,
     comb, recv_a, recv_b, fsum, xrecv, side, side_in, corner, corner_in, vert_in,
     xo, xe, own_part, yr, pleft, kright, zright, wleft, field, kern, dsum, part, pair_in, term_x,
     term_in, halo_send, halo_recv, s_send, s_recv, x_send, x_recv, f_send, f_recv,
     t_send, t_recv) = refs[9:]
    vm = (fo, fe, fr, kc, kr, br, bc)

    g = lax.axis_index("band")
    facet = lax.axis_index("facet")
    chip, core = g // 2, g % 2
    sib = {"band": 2 * chip + 1 - core}
    far = {"band": 2 * (1 - chip) + core}
    q = (facet + FGY + FGY // 2) % facets
    row, col = q // FGY, q % FGY

    def exists(d):
        r, c = row + d[0], col + d[1]
        return (r >= 0) & (r < facets // FGY) & (c >= 0) & (c < FGY)

    def device(d):
        return {"facet": (facet + FGY * d[0] + d[1] + facets) % facets}

    barrier = pltpu.get_barrier_semaphore()
    count = 2
    for d in NEIGHBOURS:
        there = exists(d)
        count = count + there.astype(jnp.int32)

        @pl.when(there)
        def _():
            pl.semaphore_signal(barrier, inc=1, device_id=device(d))

    for peer in (sib, far):
        pl.semaphore_signal(barrier, inc=1, device_id=peer)

    local = [pltpu.make_async_copy(dirty_hbm, dirty, local_sem.at[7])]
    local += [pltpu.make_async_copy(tables_hbm[i], vm[i], local_sem.at[i]) for i in range(7)]
    for copy in local:
        copy.start()

    powers = []
    for b in range(bands):
        w = offset[b]
        row_b = [jnp.float32(1.0)]
        for _ in range(1, POWERS):
            row_b.append(row_b[-1] * w)
        powers.append(row_b)

    k = psf.shape[1]
    lane = lax.broadcasted_iota(jnp.int32, (1, LANES), 1)
    comb[:, LANES:SENT, :] = jnp.zeros((8, SENT - LANES, LANES), F32)
    planes = [psf[b, :, 0, 0:LANES] for b in range(bands)]
    for s in range(POWERS):
        total = planes[0]
        if s:
            total = total * powers[0][s]
        for b in range(1, bands):
            total += planes[b] * powers[b][s]
        comb[ORDER.index(s), 0:k, :] = total
    total = jnp.zeros((k, LANES), F32)
    for b in range(bands):
        w_row = jnp.zeros((1, LANES), F32)
        for s in range(POWERS):
            w_row = jnp.where(lane == s, powers[b][s], w_row)
        total += psf[b, :, 0, LANES:k] * w_row
    comb[3, 0:k, :] = total

    h = size // 2
    side[0] = pack(coeffs[0, 0, 0:h, 0:LANES], coeffs[0, 0, h:size, 0:LANES], True)
    side[1] = pack(
        coeffs[0, 0, 0:h, size - LANES : size], coeffs[0, 0, h:size, size - LANES : size], False
    )
    for i, top in enumerate((0, size - B)):
        for j in range(2):
            lanes = slice(0, LANES) if j == 0 else slice(size - LANES, size)
            corner[2 * i + j] = pack(
                coeffs[0, 0, top : top + B // 2, lanes],
                coeffs[0, 0, top + B // 2 : top + B, lanes],
                j == 0,
            )

    def halo(d):
        dr, dc = d
        if dr == 0:
            i = (dc + 1) // 2
            src, dst = side.at[i], side_in.at[i]
        elif dc == 0:
            i = (dr + 1) // 2
            src = coeffs.at[0, 0, pl.ds(i * (size - B), B), :]
            dst = vert_in.at[i]
        else:
            i = (dr + 1) + (dc + 1) // 2
            src, dst = corner.at[i], corner_in.at[i]
        n = NEIGHBOURS.index(d)
        return pltpu.make_async_remote_copy(
            src, dst, halo_send.at[n], halo_recv.at[n], device_id=device(d)
        )

    pl.semaphore_wait(barrier, count)

    def to_sib(src, dst, i):
        return pltpu.make_async_remote_copy(src, dst, s_send.at[i], s_recv.at[i], device_id=sib)

    later = jnp.where(chip == 0, 6, 4)
    a_copies = [to_sib(comb.at[2 * (1 - core) + i], recv_a.at[i], i) for i in range(2)]
    a_copies.append(to_sib(comb.at[later + 1 - core], recv_a.at[2], 2))
    b_copies = [to_sib(comb.at[pl.ds(4 * i, 4)], recv_b.at[pl.ds(4 * i, 4)], 3 + i) for i in range(2)]
    a_copies[0].start()
    a_copies[1].start()
    for d in sorted(NEIGHBOURS, key=lambda d: abs(d[0]) + abs(d[1]) == 2):
        @pl.when(exists(d))
        def _():
            halo(d).start()

    a_copies[2].start()
    b_copies[0].start()
    b_copies[1].start()

    x_copies, f_copies = [], []
    for i in range(3):
        slot = xrecv.at[2 * core + i if i < 2 else 4 + core]
        x_copies.append(
            pltpu.make_async_remote_copy(fsum.at[i], slot, x_send.at[i], x_recv.at[i], device_id=far)
        )
        f_copies.append(
            pltpu.make_async_remote_copy(slot, slot, f_send.at[i], f_recv.at[i], device_id=sib)
        )
        a_copies[i].wait_recv()
        fsum[i] = comb[2 * core + i if i < 2 else later + core] + recv_a[i]
        x_copies[i].start()

    away, home = 2 * (1 - chip), 2 * chip
    terms = (away + 1 - core, away + core, home + 1 - core, home + core)

    def weight(b, t):
        w = powers[b]
        return jnp.where(t == 0, w[0], jnp.where(t == 1, w[1], jnp.where(t == 2, w[2], w[3])))

    kright[:, 3 * KROWS : 512] = jnp.zeros((2, 512 - 3 * KROWS, 2 * HC), BF16)
    zright[6 * HR : 1280] = jnp.zeros((1280 - 6 * HR, 2 * HC), BF16)
    put_left(xo, coeffs[0, 0])
    local[1].wait()
    own_part[...] = dot(xo[0:size], fo[...])
    local[0].wait()
    for i, t in enumerate(terms):
        total = dirty[0, 0] * weight(0, t)
        for n in range(1, bands):
            total += dirty[n, 0] * weight(n, t)
        dsum[i] = total

    for copy in local[2:]:
        copy.wait()

    for i in range(2):
        x_copies[i].wait_recv()
        f_copies[i].start()

    for d in NEIGHBOURS:
        dr, dc = d
        there = exists(d)
        incoming = halo((-dr, -dc))

        @pl.when(there)
        def _():
            incoming.wait_recv()

        if dr == 0:
            ref, i = side_in, (1 - dc) // 2
        elif dc == 0:
            ref, i = vert_in, (1 - dr) // 2
        else:
            ref, i = corner_in, (1 - dr) + (1 - dc) // 2

        @pl.when(jnp.logical_not(there))
        def _():
            ref[i] = jnp.zeros(ref.shape[1:], F32)

    def edge(right, left, m):
        top = jnp.where(m, right, left)
        bottom = pltpu.roll(jnp.where(m, left, right), LANES // 2, 1)
        return jnp.concatenate([top, bottom], axis=0)

    put_left(xe, edge(side_in[0], side_in[1], half_mask((h, LANES))))
    small = half_mask((B // 2, LANES))
    for i in range(2):
        put_left(xo, vert_in[i], size + i * B)
        put_left(xe, edge(corner_in[2 * i], corner_in[2 * i + 1], small), size + i * B)
    total_rows = size + 2 * B
    put_right(yr, own_part[...] + dot(xe[0:size], fe[...]), 0, total_rows)
    put_right(yr, dot(xo[size:], fo[...]) + dot(xe[size:], fe[...]), size, total_rows)
    full = dot(fr[...], yr[...])

    def halves(x, ref):
        cc, cs = x[:HR, :HC], x[:HR, HC:]
        sc, ss = x[HR:, :HC], x[HR:, HC:]
        ref[0] = cc - ss
        ref[1] = sc + cs
        ref[2] = cc + ss
        ref[3] = sc - cs

    halves(full, field)

    def forwarded(i):
        other = xrecv.at[2 * (1 - core) + i if i < 2 else 5 - core]
        pltpu.make_async_remote_copy(
            other, other, f_send.at[i], f_recv.at[i], device_id=sib
        ).wait_recv()

    blank = jnp.zeros((KROWS - SENT, 2 * LANES), F32)

    def kernels(first):
        column = comb[3] + recv_b[3] + xrecv[3]
        for i in range(2):
            s = g + terms[first + i]
            at = jnp.where(s < 2, s + 4, jnp.where(s < 5, s - 2, s + 1))
            slot = jnp.where(s < 2, s + 4, jnp.where(s < 5, s - 2, s - 1))
            main = comb[at] + recv_b[at] + xrecv[slot]
            last = jnp.where(lane == s, column, 0.0)
            block = jnp.concatenate([main, last], axis=1)
            put_left(pleft, jnp.concatenate([block, blank], axis=0), i * KROWS)
        both = dot(pleft[...], kc[...])
        for i in range(2):
            put_right(kright.at[i], both[i * KROWS : (i + 1) * KROWS])
            halves(dot(kr[...], kright[i]), kern.at[i])

    def term(i, put):
        a, b, c, d = (field[n] for n in range(4))
        e, f, p, r = (kern[i % 2, n] for n in range(4))
        re1, im1 = a * e - b * f, a * f + b * e
        re2, im2 = c * p - d * r, c * r + d * p
        put_right(zright, jnp.concatenate([re1 + re2, im1 - im2], axis=1), 0, 2 * HR)
        put_right(zright, jnp.concatenate([im1 + im2, re2 - re1], axis=1), HR, 2 * HR)
        put_left(wleft, dot(br[...], zright[...]))
        for j in range(2):
            rows = slice(j * h, (j + 1) * h)
            put(j, rows, dsum[i, rows] - dot(wleft[rows], bc[...]))

    def pair_copy(i, j):
        n = 2 * i + j
        rows = pl.ds(j * h, h)
        return pltpu.make_async_remote_copy(
            part.at[i, rows], pair_in.at[i, rows], t_send.at[n], t_recv.at[n], device_id=sib
        )

    def cross_copy(j):
        rows = pl.ds(j * h, h)
        return pltpu.make_async_remote_copy(
            term_x.at[rows], term_in.at[rows], t_send.at[4 + j], t_recv.at[4 + j], device_id=far
        )

    pairs = [[pair_copy(i, j) for j in range(2)] for i in range(2)]
    crosses = [cross_copy(j) for j in range(2)]

    def to_pair(i):
        def put(j, rows, value):
            part[i, rows] = value
            pairs[i][j].start()

        return put

    def to_far(j, rows, value):
        pairs[0][j].wait_recv()
        term_x[rows] = value + pair_in[0, rows]
        crosses[j].start()

    def to_out(j, rows, value):
        pairs[1][j].wait_recv()
        out[0, 0, rows] = value + pair_in[1, rows]

    forwarded(0)
    forwarded(1)
    b_copies[0].wait_recv()
    kernels(0)
    x_copies[2].wait_recv()
    f_copies[2].start()
    term(0, to_pair(0))
    term(1, to_far)
    forwarded(2)
    b_copies[1].wait_recv()
    kernels(2)
    term(2, to_pair(1))
    term(3, to_out)
    for j in range(2):
        rows = slice(j * h, (j + 1) * h)
        crosses[j].wait_recv()
        got[0, 0, rows] = term_in[rows]

    for d in NEIGHBOURS:
        @pl.when(exists(d))
        def _():
            halo(d).wait_send()

    for copy in (*a_copies, *b_copies, *x_copies, *f_copies, *pairs[0], *pairs[1], *crosses):
        copy.wait_send()


def body(coeffs, dirty, psf, band_offset):
    size = coeffs.shape[-1]
    span = size + 2 * B
    bands = dirty.shape[0]
    facets = lax.axis_size("facet")
    consts = tables(size, span, psf.shape[-1])
    vmem = pl.BlockSpec(memory_space=pltpu.VMEM)
    hbm = pl.BlockSpec(memory_space=pl.ANY)
    dma = lambda n: pltpu.SemaphoreType.DMA((n,))
    scratch = [pltpu.VMEM(c.shape, BF16) for c in consts]
    scratch += [
        pltpu.VMEM(dirty.shape, F32),
        dma(8),
        pltpu.VMEM((8, SENT, LANES), F32),
        pltpu.VMEM((3, SENT, LANES), F32),
        pltpu.VMEM((8, SENT, LANES), F32),
        pltpu.VMEM((3, SENT, LANES), F32),
        pltpu.VMEM((6, SENT, LANES), F32),
        pltpu.VMEM((2, size // 2, LANES), F32),
        pltpu.VMEM((2, size // 2, LANES), F32),
        pltpu.VMEM((4, B // 2, LANES), F32),
        pltpu.VMEM((4, B // 2, LANES), F32),
        pltpu.VMEM((2, B, size), F32),
        pltpu.VMEM((span, 3 * size), BF16),
        pltpu.VMEM((span, 3 * LANES), BF16),
        pltpu.VMEM((size, 2 * HC), F32),
        pltpu.VMEM((3 * span, 2 * HC), BF16),
        pltpu.VMEM((2 * KROWS, 6 * LANES), BF16),
        pltpu.VMEM((2, 512, 2 * HC), BF16),
        pltpu.VMEM((1280, 2 * HC), BF16),
        pltpu.VMEM((size, 6 * HC), BF16),
        pltpu.VMEM((4, HR, HC), F32),
        pltpu.VMEM((2, 4, HR, HC), F32),
        pltpu.VMEM((TERMS, size, size), F32),
        pltpu.VMEM((2, size, size), F32),
        pltpu.VMEM((2, size, size), F32),
        pltpu.VMEM((size, size), F32),
        pltpu.VMEM((size, size), F32),
        dma(8), dma(8), dma(5), dma(5), dma(3), dma(3), dma(3), dma(3), dma(6), dma(6),
    ]

    def run(*args):
        kernel(facets, size, bands, *args)

    shape = jax.ShapeDtypeStruct(coeffs.shape, F32)
    kept, received = pl.pallas_call(
        run,
        out_shape=(shape, shape),
        in_specs=[vmem, hbm, vmem, pl.BlockSpec(memory_space=pltpu.SMEM)] + [hbm] * 7,
        out_specs=(vmem, vmem),
        scratch_shapes=scratch,
        compiler_params=pltpu.CompilerParams(
            collective_id=0, has_side_effects=True, vmem_limit_bytes=56 * 1024 * 1024
        ),
        cost_estimate=pl.CostEstimate(flops=4_000_000_000, bytes_accessed=8_000_000, transcendentals=0),
    )(coeffs, dirty, psf.transpose(0, 2, 1, 3), band_offset, *[jnp.asarray(c) for c in consts])
    return kept + received


def solution(mesh):
    placed = (
        P("band", "facet", None, None),
        P("band", "facet", None, None),
        P("band", "facet", None, None),
        P("band"),
    )
    return jax.shard_map(
        body, mesh=mesh, in_specs=placed, out_specs=P("band", "facet", None, None), check_vma=False
    )
```

time: 34.1 us -> 30 us (0.88)
  local copies, waits for them, and re-layouts: 3.55 us -> 0 us
  Pallas kernels: 30.3 us -> 28.1 us
  other arithmetic: 0 us -> 1.77 us
    unnamed x2 -> x0, local copies, waits for them, and re-layouts: 3.55 us -> none
    pallas_call x1, Pallas kernels: 30.3 us -> 28.1 us  [body(): pl.pallas_call(run, out_shape=(shape, shape), in_specs=[vmem, hbm, vmem,...]
    add x0 -> x1, other arithmetic: none -> 1.77 us  [body(): return kept + received]
where the time goes in v2:
time: 30 us; the launch traced here: 29.9 us
  Pallas kernels  28.1 us (94%)
  other arithmetic  1.77 us (6%)
    pallas_call x1, Pallas kernels, body(): pl.pallas_call(run, out_shape=(shape, shape), in_specs=[vmem, hbm, vmem,...  28.1 us
    add x1, other arithmetic, body(): return kept + received  1.77 us

profile of v2, /device:TPU:0, one launch (start us, length us, event | category | flops | bytes accessed | tf_op | source)
XLA Modules:
  0.0 29.9 jit_solution(9590479959834747543)
XLA Ops:
  0.0 28.1 %shard_map.109 = (f32[1,1,256,256]{3,2,1,0:T(8,128)}, f32[1,1,256,256]{3,2,1,0:T(8,128)}) custom-call(f32[1,1,256,256]{3,2,1,0:T(8,128)} %args_0_.4, f32[4,1,256,256]{3,2,1,0:T(8,128)} %args_1_.4, f32[4,129,1,129]{3,2,1,0:T(1,128)} %bitcast.1, f32[4]{0:T(128)} %args_3_.4, bf16[768,512]{1,0:T(8,128)(2,1)} %constant.14.clone.args_4_, ...), custom_call_target="tpu_custom_call" | custom-call | flops 4000000000 | bytes 8000000 | tf_op jit(solution)/shard_map/pallas_call | solution.py:455
  28.1 1.8 %add.3 = f32[1,1,256,256]{3,2,1,0:T(8,128)} add(f32[1,1,256,256]{3,2,1,0:T(8,128)} %get-tuple-element.7, f32[1,1,256,256]{3,2,1,0:T(8,128)} %get-tuple-element.8) | non-fusion elementwise | flops 65536 | bytes 786432 | tf_op jit(solution)/shard_map/add | solution.py:466

commit v3 on v2

--- a/solution.py
+++ b/solution.py
@@ -74,21 +74,23 @@
     return hi, (x - hi.astype(F32)).astype(BF16)
 
 
-def put_left(ref, x, row=0):
-    hi, lo = split(x)
-    h, w = x.shape
-    ref[row : row + h, 0:w] = hi
-    ref[row : row + h, w : 2 * w] = hi
-    ref[row : row + h, 2 * w : 3 * w] = lo
-
-
-def put_right(ref, x, at=0, pitch=None):
-    hi, lo = split(x)
-    h = x.shape[0]
-    pitch = pitch or h
-    ref[at : at + h] = hi
-    ref[pitch + at : pitch + at + h] = lo
-    ref[2 * pitch + at : 2 * pitch + at + h] = hi
+def put_left(ref, load, height, row=0, step=16):
+    for r in range(0, height, step):
+        x = load(slice(r, r + step))
+        hi, lo = split(x)
+        w = x.shape[1]
+        rows = slice(row + r, row + r + step)
+        ref[rows, 0:w] = hi
+        ref[rows, w : 2 * w] = hi
+        ref[rows, 2 * w : 3 * w] = lo
+
+
+def put_right(ref, load, height, pitch, step=16):
+    for r in range(0, height, step):
+        hi, lo = split(load(slice(r, r + step)))
+        ref[r : r + step] = hi
+        ref[pitch + r : pitch + r + step] = lo
+        ref[2 * pitch + r : 2 * pitch + r + step] = hi
 
 
 def dot(a, b):
@@ -107,11 +109,11 @@
 
 def kernel(
     facets, size, bands,
-    coeffs, dirty_hbm, psf, offset, *refs,
+    coeffs_hbm, dirty_hbm, psf_hbm, offset, *refs,
 ):
     tables_hbm = refs[:7]
     out, got = refs[7:9]
-    (fo, fe, fr, kc, kr, br, bc, dirty, local_sem,
+    (fo, fe, fr, kc, kr, br, bc, coeffs, dirty, psf, acc, kacc, local_sem,
      comb, recv_a, recv_b, fsum, xrecv, side, side_in, corner, corner_in, vert_in,
      xo, xe, own_part, yr, pleft, kright, zright, wleft, field, kern, dsum, part, pair_in, term_x,
      term_in, halo_send, halo_recv, s_send, s_recv, x_send, x_recv, f_send, f_recv,
@@ -133,6 +135,13 @@
     def device(d):
         return {"facet": (facet + FGY * d[0] + d[1] + facets) % facets}
 
+    inputs = [
+        pltpu.make_async_copy(psf_hbm, psf, local_sem.at[8]),
+        pltpu.make_async_copy(coeffs_hbm, coeffs, local_sem.at[9]),
+    ]
+    for copy in inputs:
+        copy.start()
+
     barrier = pltpu.get_barrier_semaphore()
     count = 2
     for d in NEIGHBOURS:
@@ -162,23 +171,30 @@
     k = psf.shape[1]
     lane = lax.broadcasted_iota(jnp.int32, (1, LANES), 1)
     comb[:, LANES:SENT, :] = jnp.zeros((8, SENT - LANES, LANES), F32)
-    planes = [psf[b, :, 0, 0:LANES] for b in range(bands)]
-    for s in range(POWERS):
-        total = planes[0]
-        if s:
-            total = total * powers[0][s]
-        for b in range(1, bands):
-            total += planes[b] * powers[b][s]
-        comb[ORDER.index(s), 0:k, :] = total
-    total = jnp.zeros((k, LANES), F32)
+    w_rows = []
     for b in range(bands):
         w_row = jnp.zeros((1, LANES), F32)
         for s in range(POWERS):
             w_row = jnp.where(lane == s, powers[b][s], w_row)
-        total += psf[b, :, 0, LANES:k] * w_row
-    comb[3, 0:k, :] = total
+        w_rows.append(w_row)
+    inputs[0].wait()
+    for top in range(0, k, 32):
+        rows = slice(top, min(top + 32, k))
+        planes = [psf[b, rows, 0, 0:LANES] for b in range(bands)]
+        for s in range(POWERS):
+            total = planes[0]
+            if s:
+                total = total * powers[0][s]
+            for b in range(1, bands):
+                total += planes[b] * powers[b][s]
+            comb[ORDER.index(s), rows, :] = total
+        total = psf[0, rows, 0, LANES:k] * w_rows[0]
+        for b in range(1, bands):
+            total += psf[b, rows, 0, LANES:k] * w_rows[b]
+        comb[3, rows, :] = total
 
     h = size // 2
+    inputs[1].wait()
     side[0] = pack(coeffs[0, 0, 0:h, 0:LANES], coeffs[0, 0, h:size, 0:LANES], True)
     side[1] = pack(
         coeffs[0, 0, 0:h, size - LANES : size], coeffs[0, 0, h:size, size - LANES : size], False
@@ -251,15 +267,18 @@
 
     kright[:, 3 * KROWS : 512] = jnp.zeros((2, 512 - 3 * KROWS, 2 * HC), BF16)
     zright[6 * HR : 1280] = jnp.zeros((1280 - 6 * HR, 2 * HC), BF16)
-    put_left(xo, coeffs[0, 0])
+    put_left(xo, lambda rows: coeffs[0, 0, rows], size)
     local[1].wait()
     own_part[...] = dot(xo[0:size], fo[...])
     local[0].wait()
-    for i, t in enumerate(terms):
-        total = dirty[0, 0] * weight(0, t)
-        for n in range(1, bands):
-            total += dirty[n, 0] * weight(n, t)
-        dsum[i] = total
+    for r in range(0, size, 32):
+        rows = slice(r, r + 32)
+        planes = [dirty[n, 0, rows] for n in range(bands)]
+        for i, t in enumerate(terms):
+            total = planes[0] * weight(0, t)
+            for n in range(1, bands):
+                total += planes[n] * weight(n, t)
+            dsum[i, rows] = total
 
     for copy in local[2:]:
         copy.wait()
@@ -293,25 +312,30 @@
         bottom = pltpu.roll(jnp.where(m, left, right), LANES // 2, 1)
         return jnp.concatenate([top, bottom], axis=0)
 
-    put_left(xe, edge(side_in[0], side_in[1], half_mask((h, LANES))))
+    def place(ref, x, row, step):
+        put_left(ref, lambda rows: x[rows], x.shape[0], row, step)
+
+    place(xe, edge(side_in[0], side_in[1], half_mask((h, LANES))), 0, 64)
     small = half_mask((B // 2, LANES))
     for i in range(2):
-        put_left(xo, vert_in[i], size + i * B)
-        put_left(xe, edge(corner_in[2 * i], corner_in[2 * i + 1], small), size + i * B)
+        put_left(xo, lambda rows: vert_in[i, rows], B, size + i * B)
+        place(xe, edge(corner_in[2 * i], corner_in[2 * i + 1], small), size + i * B, 64)
     total_rows = size + 2 * B
-    put_right(yr, own_part[...] + dot(xe[0:size], fe[...]), 0, total_rows)
-    put_right(yr, dot(xo[size:], fo[...]) + dot(xe[size:], fe[...]), size, total_rows)
-    full = dot(fr[...], yr[...])
-
-    def halves(x, ref):
-        cc, cs = x[:HR, :HC], x[:HR, HC:]
-        sc, ss = x[HR:, :HC], x[HR:, HC:]
-        ref[0] = cc - ss
-        ref[1] = sc + cs
-        ref[2] = cc + ss
-        ref[3] = sc - cs
-
-    halves(full, field)
+    acc[0:size] = own_part[...] + dot(xe[0:size], fe[...])
+    acc[size:total_rows] = dot(xo[size:], fo[...]) + dot(xe[size:], fe[...])
+    put_right(yr, lambda rows: acc[rows], total_rows, total_rows)
+    acc[...] = dot(fr[...], yr[...])
+
+    def halves(load, rows):
+        below = slice(HR + rows.start, HR + rows.stop)
+        cc, cs = load(rows, slice(0, HC)), load(rows, slice(HC, 2 * HC))
+        sc, ss = load(below, slice(0, HC)), load(below, slice(HC, 2 * HC))
+        return cc - ss, sc + cs, cc + ss, sc - cs
+
+    for r in range(0, HR, 16):
+        rows = slice(r, r + 16)
+        for n, x in enumerate(halves(lambda a, b: acc[a, b], rows)):
+            field[n, rows] = x
 
     def forwarded(i):
         other = xrecv.at[2 * (1 - core) + i if i < 2 else 5 - core]
@@ -330,20 +354,34 @@
             main = comb[at] + recv_b[at] + xrecv[slot]
             last = jnp.where(lane == s, column, 0.0)
             block = jnp.concatenate([main, last], axis=1)
-            put_left(pleft, jnp.concatenate([block, blank], axis=0), i * KROWS)
-        both = dot(pleft[...], kc[...])
+            place(pleft, jnp.concatenate([block, blank], axis=0), i * KROWS, 16)
+        kacc[...] = dot(pleft[...], kc[...])
         for i in range(2):
-            put_right(kright.at[i], both[i * KROWS : (i + 1) * KROWS])
-            halves(dot(kr[...], kright[i]), kern.at[i])
+            put_right(
+                kright.at[i],
+                lambda rows: kacc[i * KROWS + rows.start : i * KROWS + rows.stop],
+                KROWS, KROWS,
+            )
+            kern[i] = dot(kr[...], kright[i])
 
     def term(i, put):
-        a, b, c, d = (field[n] for n in range(4))
-        e, f, p, r = (kern[i % 2, n] for n in range(4))
-        re1, im1 = a * e - b * f, a * f + b * e
-        re2, im2 = c * p - d * r, c * r + d * p
-        put_right(zright, jnp.concatenate([re1 + re2, im1 - im2], axis=1), 0, 2 * HR)
-        put_right(zright, jnp.concatenate([im1 + im2, re2 - re1], axis=1), HR, 2 * HR)
-        put_left(wleft, dot(br[...], zright[...]))
+        for r in range(0, HR, 16):
+            rows = slice(r, r + 16)
+            a, b, c, d = (field[n, rows] for n in range(4))
+            e, f, p, q = halves(lambda u, v: kern[i % 2, u, v], rows)
+            re1, im1 = a * e - b * f, a * f + b * e
+            re2, im2 = c * p - d * q, c * q + d * p
+            parts = ((re1 + re2, im1 - im2), (im1 + im2, re2 - re1))
+            for m in range(2):
+                for n in range(2):
+                    hi, lo = split(parts[m][n])
+                    lanes = slice(n * HC, (n + 1) * HC)
+                    at = m * HR + r
+                    zright[at : at + 16, lanes] = hi
+                    zright[2 * HR + at : 2 * HR + at + 16, lanes] = lo
+                    zright[4 * HR + at : 4 * HR + at + 16, lanes] = hi
+        acc[0:size] = dot(br[...], zright[...])
+        put_left(wleft, lambda rows: acc[rows], size)
         for j in range(2):
             rows = slice(j * h, (j + 1) * h)
             put(j, rows, dsum[i, rows] - dot(wleft[rows], bc[...]))
@@ -411,15 +449,20 @@
     size = coeffs.shape[-1]
     span = size + 2 * B
     bands = dirty.shape[0]
+    psf = psf.transpose(0, 2, 1, 3)
     facets = lax.axis_size("facet")
     consts = tables(size, span, psf.shape[-1])
     vmem = pl.BlockSpec(memory_space=pltpu.VMEM)
-    hbm = pl.BlockSpec(memory_space=pl.ANY)
+    hbm = pl.BlockSpec(memory_space=pltpu.HBM)
     dma = lambda n: pltpu.SemaphoreType.DMA((n,))
     scratch = [pltpu.VMEM(c.shape, BF16) for c in consts]
     scratch += [
+        pltpu.VMEM(coeffs.shape, F32),
         pltpu.VMEM(dirty.shape, F32),
-        dma(8),
+        pltpu.VMEM(psf.shape, F32),
+        pltpu.VMEM((2 * HR, 2 * HC), F32),
+        pltpu.VMEM((2 * KROWS, 2 * HC), F32),
+        dma(10),
         pltpu.VMEM((8, SENT, LANES), F32),
         pltpu.VMEM((3, SENT, LANES), F32),
         pltpu.VMEM((8, SENT, LANES), F32),
@@ -439,7 +482,7 @@
         pltpu.VMEM((1280, 2 * HC), BF16),
         pltpu.VMEM((size, 6 * HC), BF16),
         pltpu.VMEM((4, HR, HC), F32),
-        pltpu.VMEM((2, 4, HR, HC), F32),
+        pltpu.VMEM((2, 2 * HR, 2 * HC), F32),
         pltpu.VMEM((TERMS, size, size), F32),
         pltpu.VMEM((2, size, size), F32),
         pltpu.VMEM((2, size, size), F32),
@@ -455,14 +498,14 @@
     kept, received = pl.pallas_call(
         run,
         out_shape=(shape, shape),
-        in_specs=[vmem, hbm, vmem, pl.BlockSpec(memory_space=pltpu.SMEM)] + [hbm] * 7,
+        in_specs=[hbm, hbm, hbm, pl.BlockSpec(memory_space=pltpu.SMEM)] + [hbm] * 7,
         out_specs=(vmem, vmem),
         scratch_shapes=scratch,
         compiler_params=pltpu.CompilerParams(
-            collective_id=0, has_side_effects=True, vmem_limit_bytes=56 * 1024 * 1024
+            collective_id=0, has_side_effects=True, vmem_limit_bytes=24 * 1024 * 1024
         ),
         cost_estimate=pl.CostEstimate(flops=4_000_000_000, bytes_accessed=8_000_000, transcendentals=0),
-    )(coeffs, dirty, psf.transpose(0, 2, 1, 3), band_offset, *[jnp.asarray(c) for c in consts])
+    )(coeffs, dirty, psf, band_offset, *[jnp.asarray(c) for c in consts])
     return kept + received
 
 

time: 30 us -> 40.2 us (1.34); the launches traced: 29.9 us -> 39.7 us
  local copies, waits for them, and re-layouts: 0 us -> 11.6 us
  other arithmetic: 1.77 us -> 0.74 us
  Pallas kernels: 28.1 us -> 27.4 us
    unnamed x0 -> x22, local copies, waits for them, and re-layouts: none -> 11.6 us
    add x1, other arithmetic: 1.77 us -> 0.74 us  [body(): return kept + received]
    pallas_call x1, Pallas kernels: 28.1 us -> 27.4 us  [body(): pl.pallas_call(run, out_shape=(shape, shape), in_specs=[hbm, hbm, hbm, pl...]
where the time goes in v3:
time: 40.2 us; the launch traced here: 39.7 us
  Pallas kernels  27.4 us (68%)
  local copies, waits for them, and re-layouts  11.6 us (29%)
  other arithmetic  0.74 us (2%)
    pallas_call x1, Pallas kernels, body(): pl.pallas_call(run, out_shape=(shape, shape), in_specs=[hbm, hbm, hbm, pl...  27.4 us
    unnamed x22, local copies, waits for them, and re-layouts  11.6 us

profile of v3, /device:TPU:0, one launch (start us, length us, event | category | flops | bytes accessed | tf_op | source)
XLA Modules:
  0.0 39.7 jit_solution(11871164391803323787)
XLA Ops:
  0.0 0.0 copy-start.3
  0.0 0.7 %copy-done.3 = f32[4]{0:T(128)S(1)} copy-done((f32[4]{0:T(128)S(1)}, f32[4]{0:T(128)}, u32[]{:S(2)}) %copy-start.3) | copy-done | bytes 40
  0.7 0.0 copy-start
  0.7 1.2 %copy-done = f32[4,1,256,256]{3,2,1,0:T(8,128)S(1)} copy-done((f32[4,1,256,256]{3,2,1,0:T(8,128)S(1)}, f32[4,1,256,256]{3,2,1,0:T(8,128)}, u32[]{:S(2)}) %copy-start) | copy-done | bytes 1048600
  1.9 0.0 copy-start.1
  1.9 1.0 %copy-done.1 = f32[4,1,129,129]{3,1,2,0:T(1,128)S(1)} copy-done((f32[4,1,129,129]{3,1,2,0:T(1,128)S(1)}, f32[4,1,129,129]{3,1,2,0:T(1,128)}, u32[]{:S(2)}) %copy-start.1) | copy-done | bytes 266280
  2.9 0.0 copy-start.2
  2.9 0.9 %copy-done.2 = f32[1,1,256,256]{3,2,1,0:T(8,128)S(1)} copy-done((f32[1,1,256,256]{3,2,1,0:T(8,128)S(1)}, f32[1,1,256,256]{3,2,1,0:T(8,128)}, u32[]{:S(2)}) %copy-start.2) | copy-done | bytes 262168
  3.9 0.0 copy-start.4
  3.9 1.2 %copy-done.4 = bf16[416,1152]{1,0:T(8,128)(2,1)S(1)} copy-done((bf16[416,1152]{1,0:T(8,128)(2,1)S(1)}, bf16[416,1152]{1,0:T(8,128)(2,1)}, u32[]{:S(2)}) %copy-start.4) | copy-done | bytes 958488
  5.1 0.0 copy-start.5
  5.1 1.1 %copy-done.5 = bf16[1536,256]{1,0:T(8,128)(2,1)S(1)} copy-done((bf16[1536,256]{1,0:T(8,128)(2,1)S(1)}, bf16[1536,256]{1,0:T(8,128)(2,1)}, u32[]{:S(2)}) %copy-start.5) | copy-done | bytes 786456
  6.2 0.0 copy-start.6
  6.2 1.1 %copy-done.6 = bf16[768,512]{1,0:T(8,128)(2,1)S(1)} copy-done((bf16[768,512]{1,0:T(8,128)(2,1)S(1)}, bf16[768,512]{1,0:T(8,128)(2,1)}, u32[]{:S(2)}) %copy-start.6) | copy-done | bytes 786456
  7.3 0.0 copy-start.7
  7.3 1.1 %copy-done.7 = bf16[768,512]{1,0:T(8,128)(2,1)S(1)} copy-done((bf16[768,512]{1,0:T(8,128)(2,1)S(1)}, bf16[768,512]{1,0:T(8,128)(2,1)}, u32[]{:S(2)}) %copy-start.7) | copy-done | bytes 786456
  8.5 0.0 copy-start.8
  8.5 1.1 %copy-done.8 = bf16[256,1280]{1,0:T(8,128)(2,1)S(1)} copy-done((bf16[256,1280]{1,0:T(8,128)(2,1)S(1)}, bf16[256,1280]{1,0:T(8,128)(2,1)}, u32[]{:S(2)}) %copy-start.8) | copy-done | bytes 655384
  9.6 0.0 copy-start.9
  9.6 1.0 %copy-done.9 = bf16[416,512]{1,0:T(8,128)(2,1)S(1)} copy-done((bf16[416,512]{1,0:T(8,128)(2,1)S(1)}, bf16[416,512]{1,0:T(8,128)(2,1)}, u32[]{:S(2)}) %copy-start.9) | copy-done | bytes 426008
  10.6 0.0 copy-start.10
  10.6 1.0 %copy-done.10 = bf16[384,512]{1,0:T(8,128)(2,1)S(1)} copy-done((bf16[384,512]{1,0:T(8,128)(2,1)S(1)}, bf16[384,512]{1,0:T(8,128)(2,1)}, u32[]{:S(2)}) %copy-start.10) | copy-done | bytes 393240
  11.6 27.4 %shard_map.109 = (f32[1,1,256,256]{3,2,1,0:T(8,128)S(1)}, f32[1,1,256,256]{3,2,1,0:T(8,128)S(1)}) custom-call(f32[1,1,256,256]{3,2,1,0:T(8,128)S(1)} %copy-done.2, f32[4,1,256,256]{3,2,1,0:T(8,128)S(1)} %copy-done, f32[4,129,1,129]{3,2,1,0:T(1,128)S(1)} %bitcast.1, f32[4]{0:T(128)S(1)} %copy-done.3, bf16[768,512]{1,0:T(8,128)(2,1)S(1)} %copy-done.7, ...), custom_call_target="tpu_custom_call" | custom-call | flops 4000000000 | bytes 8000000 | tf_op jit(solution)/shard_map/pallas_call | solution.py:498
  38.9 0.7 %add.3 = f32[1,1,256,256]{3,2,1,0:T(8,128)} add(f32[1,1,256,256]{3,2,1,0:T(8,128)S(1)} %get-tuple-element.7, f32[1,1,256,256]{3,2,1,0:T(8,128)S(1)} %get-tuple-element.8) | non-fusion elementwise | flops 65536 | bytes 786432 | tf_op jit(solution)/shard_map/add | solution.py:509
Async XLA Ops:
  0.0 0.7 %copy-start.3 = (f32[4]{0:T(128)S(1)}, f32[4]{0:T(128)}, u32[]{:S(2)}) copy-start(f32[4]{0:T(128)} %args_3_.4) | copy-start | bytes 52
  0.7 1.2 %copy-start = (f32[4,1,256,256]{3,2,1,0:T(8,128)S(1)}, f32[4,1,256,256]{3,2,1,0:T(8,128)}, u32[]{:S(2)}) copy-start(f32[4,1,256,256]{3,2,1,0:T(8,128)} %args_1_.4) | copy-start | bytes 3145732
  1.9 1.0 %copy-start.1 = (f32[4,1,129,129]{3,1,2,0:T(1,128)S(1)}, f32[4,1,129,129]{3,1,2,0:T(1,128)}, u32[]{:S(2)}) copy-start(f32[4,1,129,129]{3,1,2,0:T(1,128)} %param.13) | copy-start | bytes 798772
  2.9 0.9 %copy-start.2 = (f32[1,1,256,256]{3,2,1,0:T(8,128)S(1)}, f32[1,1,256,256]{3,2,1,0:T(8,128)}, u32[]{:S(2)}) copy-start(f32[1,1,256,256]{3,2,1,0:T(8,128)} %args_0_.4) | copy-start | bytes 786436
  3.9 1.2 %copy-start.4 = (bf16[416,1152]{1,0:T(8,128)(2,1)S(1)}, bf16[416,1152]{1,0:T(8,128)(2,1)}, u32[]{:S(2)}) copy-start(bf16[416,1152]{1,0:T(8,128)(2,1)} %constant.16.clone.args_6_) | copy-start | bytes 2875396
  5.1 1.1 %copy-start.5 = (bf16[1536,256]{1,0:T(8,128)(2,1)S(1)}, bf16[1536,256]{1,0:T(8,128)(2,1)}, u32[]{:S(2)}) copy-start(bf16[1536,256]{1,0:T(8,128)(2,1)} %constant.20.clone.args_10_) | copy-start | bytes 2359300
  6.2 1.1 %copy-start.6 = (bf16[768,512]{1,0:T(8,128)(2,1)S(1)}, bf16[768,512]{1,0:T(8,128)(2,1)}, u32[]{:S(2)}) copy-start(bf16[768,512]{1,0:T(8,128)(2,1)} %constant.17.clone.args_7_) | copy-start | bytes 2359300
  7.3 1.1 %copy-start.7 = (bf16[768,512]{1,0:T(8,128)(2,1)S(1)}, bf16[768,512]{1,0:T(8,128)(2,1)}, u32[]{:S(2)}) copy-start(bf16[768,512]{1,0:T(8,128)(2,1)} %constant.14.clone.args_4_) | copy-start | bytes 2359300
  8.5 1.1 %copy-start.8 = (bf16[256,1280]{1,0:T(8,128)(2,1)S(1)}, bf16[256,1280]{1,0:T(8,128)(2,1)}, u32[]{:S(2)}) copy-start(bf16[256,1280]{1,0:T(8,128)(2,1)} %constant.19.clone.args_9_) | copy-start | bytes 1966084
  9.6 1.0 %copy-start.9 = (bf16[416,512]{1,0:T(8,128)(2,1)S(1)}, bf16[416,512]{1,0:T(8,128)(2,1)}, u32[]{:S(2)}) copy-start(bf16[416,512]{1,0:T(8,128)(2,1)} %constant.18.clone.args_8_) | copy-start | bytes 1277956
  10.6 1.0 %copy-start.10 = (bf16[384,512]{1,0:T(8,128)(2,1)S(1)}, bf16[384,512]{1,0:T(8,128)(2,1)}, u32[]{:S(2)}) copy-start(bf16[384,512]{1,0:T(8,128)(2,1)} %constant.15.clone.args_5_) | copy-start | bytes 1179652

commit v4 on v3

--- a/solution.py
+++ b/solution.py
@@ -177,21 +177,22 @@
         for s in range(POWERS):
             w_row = jnp.where(lane == s, powers[b][s], w_row)
         w_rows.append(w_row)
-    inputs[0].wait()
-    for top in range(0, k, 32):
-        rows = slice(top, min(top + 32, k))
-        planes = [psf[b, rows, 0, 0:LANES] for b in range(bands)]
-        for s in range(POWERS):
-            total = planes[0]
-            if s:
-                total = total * powers[0][s]
-            for b in range(1, bands):
-                total += planes[b] * powers[b][s]
-            comb[ORDER.index(s), rows, :] = total
-        total = psf[0, rows, 0, LANES:k] * w_rows[0]
-        for b in range(1, bands):
-            total += psf[b, rows, 0, LANES:k] * w_rows[b]
-        comb[3, rows, :] = total
+    def combine(wanted, with_last):
+        for top in range(0, k, 32):
+            rows = slice(top, min(top + 32, k))
+            planes = [psf[b, rows, 0, 0:LANES] for b in range(bands)]
+            for s in wanted:
+                total = planes[0]
+                if s:
+                    total = total * powers[0][s]
+                for b in range(1, bands):
+                    total += planes[b] * powers[b][s]
+                comb[ORDER.index(s), rows, :] = total
+            if with_last:
+                total = psf[0, rows, 0, LANES:k] * w_rows[0]
+                for b in range(1, bands):
+                    total += psf[b, rows, 0, LANES:k] * w_rows[b]
+                comb[3, rows, :] = total
 
     h = size // 2
     inputs[1].wait()
@@ -225,6 +226,8 @@
             src, dst, halo_send.at[n], halo_recv.at[n], device_id=device(d)
         )
 
+    inputs[0].wait()
+    combine((2, 3, 4), True)
     pl.semaphore_wait(barrier, count)
 
     def to_sib(src, dst, i):
@@ -241,12 +244,9 @@
         def _():
             halo(d).start()
 
-    a_copies[2].start()
-    b_copies[0].start()
-    b_copies[1].start()
-
     x_copies, f_copies = [], []
-    for i in range(3):
+
+    def cross_kernel(i):
         slot = xrecv.at[2 * core + i if i < 2 else 4 + core]
         x_copies.append(
             pltpu.make_async_remote_copy(fsum.at[i], slot, x_send.at[i], x_recv.at[i], device_id=far)
@@ -257,6 +257,14 @@
         a_copies[i].wait_recv()
         fsum[i] = comb[2 * core + i if i < 2 else later + core] + recv_a[i]
         x_copies[i].start()
+
+    cross_kernel(0)
+    cross_kernel(1)
+    combine((0, 1, 5, 6), False)
+    a_copies[2].start()
+    b_copies[0].start()
+    b_copies[1].start()
+    cross_kernel(2)
 
     away, home = 2 * (1 - chip), 2 * chip
     terms = (away + 1 - core, away + core, home + 1 - core, home + core)
@@ -502,7 +510,7 @@
         out_specs=(vmem, vmem),
         scratch_shapes=scratch,
         compiler_params=pltpu.CompilerParams(
-            collective_id=0, has_side_effects=True, vmem_limit_bytes=24 * 1024 * 1024
+            collective_id=0, has_side_effects=True, vmem_limit_bytes=54592 * 1024
         ),
         cost_estimate=pl.CostEstimate(flops=4_000_000_000, bytes_accessed=8_000_000, transcendentals=0),
     )(coeffs, dirty, psf, band_offset, *[jnp.asarray(c) for c in consts])

time: 40.2 us -> 27.8 us (0.69); the launches traced: 39.7 us -> 27.7 us
  local copies, waits for them, and re-layouts: 11.6 us -> 0.65 us
  Pallas kernels: 27.4 us -> 26.3 us
    unnamed x22 -> x2, local copies, waits for them, and re-layouts: 11.6 us -> 0.65 us
    pallas_call x1, Pallas kernels: 27.4 us -> 26.3 us  [body(): pl.pallas_call(run, out_shape=(shape, shape), in_specs=[hbm, hbm, hbm, pl...]
where the time goes in v4:
time: 27.8 us; the launch traced here: 27.7 us
  Pallas kernels  26.3 us (95%)
  other arithmetic  0.74 us (3%)
  local copies, waits for them, and re-layouts  0.65 us (2%)
    pallas_call x1, Pallas kernels, body(): pl.pallas_call(run, out_shape=(shape, shape), in_specs=[hbm, hbm, hbm, pl...  26.3 us
    add x1, other arithmetic, body(): return kept + received  0.74 us
    unnamed x2, local copies, waits for them, and re-layouts  0.65 us

profile of v4, /device:TPU:0, one launch (start us, length us, event | category | flops | bytes accessed | tf_op | source)
XLA Modules:
  0.0 27.7 jit_solution(14705303055918844520)
XLA Ops:
  0.0 0.0 copy-start
  0.0 0.7 %copy-done = f32[4]{0:T(128)S(1)} copy-done((f32[4]{0:T(128)S(1)}, f32[4]{0:T(128)}, u32[]{:S(2)}) %copy-start) | copy-done | bytes 40
  0.7 26.3 %shard_map.109 = (f32[1,1,256,256]{3,2,1,0:T(8,128)S(1)}, f32[1,1,256,256]{3,2,1,0:T(8,128)S(1)}) custom-call(f32[1,1,256,256]{3,2,1,0:T(8,128)} %args_0_.4, f32[4,1,256,256]{3,2,1,0:T(8,128)} %args_1_.4, f32[4,129,1,129]{3,2,1,0:T(1,128)} %bitcast.1, f32[4]{0:T(128)S(1)} %copy-done, bf16[768,512]{1,0:T(8,128)(2,1)} %constant.14.clone.args_4_, ...), custom_call_target="tpu_custom_call" | custom-call | flops 4000000000 | bytes 8000000 | tf_op jit(solution)/shard_map/pallas_call | solution.py:506
  26.9 0.7 %add.3 = f32[1,1,256,256]{3,2,1,0:T(8,128)} add(f32[1,1,256,256]{3,2,1,0:T(8,128)S(1)} %get-tuple-element.7, f32[1,1,256,256]{3,2,1,0:T(8,128)S(1)} %get-tuple-element.8) | non-fusion elementwise | flops 65536 | bytes 786432 | tf_op jit(solution)/shard_map/add | solution.py:517
Async XLA Ops:
  0.0 0.7 %copy-start = (f32[4]{0:T(128)S(1)}, f32[4]{0:T(128)}, u32[]{:S(2)}) copy-start(f32[4]{0:T(128)} %args_3_.4) | copy-start | bytes 52

commit v5 on v4

--- a/solution.py
+++ b/solution.py
@@ -11,11 +11,15 @@
 TERMS = 4
 FGY = 4
 POWERS = 2 * TERMS - 1
-ORDER = (2, 3, 4, None, 0, 1, 5, 6)
+EARLY = (2, 3, 4)
+LATE = (0, 1, 5, 6)
 HR = 208
 HC = 256
 KROWS = 144
 SENT = 136
+TURNED = 3 * SENT
+SHARE = 216
+PIECES = ((0, 112), (112, 104))
 LANES = 128
 F32 = jnp.float32
 BF16 = jnp.bfloat16
@@ -114,7 +118,8 @@
     tables_hbm = refs[:7]
     out, got = refs[7:9]
     (fo, fe, fr, kc, kr, br, bc, coeffs, dirty, psf, acc, kacc, local_sem,
-     comb, recv_a, recv_b, fsum, xrecv, side, side_in, corner, corner_in, vert_in,
+     early, early_a, early_b, early_sum, early_x, late, late_a, late_b, late_sum, late_x, last,
+     side, side_in, corner, corner_in, vert_in,
      xo, xe, own_part, yr, pleft, kright, zright, wleft, field, kern, dsum, part, pair_in, term_x,
      term_in, halo_send, halo_recv, s_send, s_recv, x_send, x_recv, f_send, f_recv,
      t_send, t_recv) = refs[9:]
@@ -170,7 +175,13 @@
 
     k = psf.shape[1]
     lane = lax.broadcasted_iota(jnp.int32, (1, LANES), 1)
-    comb[:, LANES:SENT, :] = jnp.zeros((8, SENT - LANES, LANES), F32)
+    tail = jnp.zeros((SENT - LANES, LANES), F32)
+    for i in range(3):
+        early[i * SENT + LANES : (i + 1) * SENT] = tail
+    early[TURNED + 16 :] = jnp.zeros((2 * SHARE - TURNED - 16, LANES), F32)
+    for i in range(4):
+        late[i, LANES:SENT] = tail
+    last[LANES:SENT] = tail
     w_rows = []
     for b in range(bands):
         w_row = jnp.zeros((1, LANES), F32)
@@ -187,12 +198,16 @@
                     total = total * powers[0][s]
                 for b in range(1, bands):
                     total += planes[b] * powers[b][s]
-                comb[ORDER.index(s), rows, :] = total
+                if s in EARLY:
+                    at = EARLY.index(s) * SENT
+                    early[at + rows.start : at + rows.stop] = total
+                else:
+                    late[LATE.index(s), rows] = total
             if with_last:
                 total = psf[0, rows, 0, LANES:k] * w_rows[0]
                 for b in range(1, bands):
                     total += psf[b, rows, 0, LANES:k] * w_rows[b]
-                comb[3, rows, :] = total
+                last[rows] = total
 
     h = size // 2
     inputs[1].wait()
@@ -227,16 +242,23 @@
         )
 
     inputs[0].wait()
-    combine((2, 3, 4), True)
+    combine(EARLY, True)
+    early[TURNED : TURNED + 8] = jnp.transpose(last[0:LANES])[0:8]
+    early[TURNED + 8 : TURNED + 16] = last[LANES:SENT]
     pl.semaphore_wait(barrier, count)
 
     def to_sib(src, dst, i):
         return pltpu.make_async_remote_copy(src, dst, s_send.at[i], s_recv.at[i], device_id=sib)
 
-    later = jnp.where(chip == 0, 6, 4)
-    a_copies = [to_sib(comb.at[2 * (1 - core) + i], recv_a.at[i], i) for i in range(2)]
-    a_copies.append(to_sib(comb.at[later + 1 - core], recv_a.at[2], 2))
-    b_copies = [to_sib(comb.at[pl.ds(4 * i, 4)], recv_b.at[pl.ds(4 * i, 4)], 3 + i) for i in range(2)]
+    away_late = jnp.where(chip == 0, 2, 0)
+
+    def piece(i, who):
+        at, rows = PIECES[i]
+        return pl.ds(pl.multiple_of(SHARE * who + at, 8), rows)
+
+    a_copies = [to_sib(early.at[piece(i, 1 - core)], early_a.at[piece(i, 0)], i) for i in range(2)]
+    a_copies.append(to_sib(late.at[away_late + 1 - core], late_a, 2))
+    b_copies = [to_sib(early, early_b, 3), to_sib(late, late_b, 4)]
     a_copies[0].start()
     a_copies[1].start()
     for d in sorted(NEIGHBOURS, key=lambda d: abs(d[0]) + abs(d[1]) == 2):
@@ -245,26 +267,24 @@
             halo(d).start()
 
     x_copies, f_copies = [], []
-
-    def cross_kernel(i):
-        slot = xrecv.at[2 * core + i if i < 2 else 4 + core]
+    for i in range(3):
+        src, slot = late_sum, late_x.at[core]
+        if i < 2:
+            src, slot = early_sum.at[piece(i, 0)], early_x.at[piece(i, core)]
         x_copies.append(
-            pltpu.make_async_remote_copy(fsum.at[i], slot, x_send.at[i], x_recv.at[i], device_id=far)
+            pltpu.make_async_remote_copy(src, slot, x_send.at[i], x_recv.at[i], device_id=far)
         )
         f_copies.append(
             pltpu.make_async_remote_copy(slot, slot, f_send.at[i], f_recv.at[i], device_id=sib)
         )
+    for i in range(2):
         a_copies[i].wait_recv()
-        fsum[i] = comb[2 * core + i if i < 2 else later + core] + recv_a[i]
+        early_sum[piece(i, 0)] = early[piece(i, core)] + early_a[piece(i, 0)]
         x_copies[i].start()
-
-    cross_kernel(0)
-    cross_kernel(1)
-    combine((0, 1, 5, 6), False)
+    combine(LATE, False)
     a_copies[2].start()
     b_copies[0].start()
     b_copies[1].start()
-    cross_kernel(2)
 
     away, home = 2 * (1 - chip), 2 * chip
     terms = (away + 1 - core, away + core, home + 1 - core, home + core)
@@ -295,6 +315,10 @@
         x_copies[i].wait_recv()
         f_copies[i].start()
 
+    a_copies[2].wait_recv()
+    late_sum[...] = late[away_late + core] + late_a[...]
+    x_copies[2].start()
+
     for d in NEIGHBOURS:
         dr, dc = d
         there = exists(d)
@@ -346,7 +370,7 @@
             field[n, rows] = x
 
     def forwarded(i):
-        other = xrecv.at[2 * (1 - core) + i if i < 2 else 5 - core]
+        other = early_x.at[piece(i, 1 - core)] if i < 2 else late_x.at[1 - core]
         pltpu.make_async_remote_copy(
             other, other, f_send.at[i], f_recv.at[i], device_id=sib
         ).wait_recv()
@@ -354,14 +378,21 @@
     blank = jnp.zeros((KROWS - SENT, 2 * LANES), F32)
 
     def kernels(first):
-        column = comb[3] + recv_b[3] + xrecv[3]
+        turned = slice(TURNED, TURNED + 16)
+        turned = early[turned] + early_b[turned] + early_x[turned]
+        square = jnp.concatenate([turned[0:8], jnp.zeros((LANES - 8, LANES), F32)], axis=0)
+        column = jnp.concatenate([jnp.transpose(square), turned[8:16]], axis=0)
         for i in range(2):
             s = g + terms[first + i]
-            at = jnp.where(s < 2, s + 4, jnp.where(s < 5, s - 2, s + 1))
-            slot = jnp.where(s < 2, s + 4, jnp.where(s < 5, s - 2, s - 1))
-            main = comb[at] + recv_b[at] + xrecv[slot]
-            last = jnp.where(lane == s, column, 0.0)
-            block = jnp.concatenate([main, last], axis=1)
+            near = jnp.clip(s, 2, 4) if first else s
+            rows = pl.ds(pl.multiple_of((near - 2) * SENT, 8), SENT)
+            main = early[rows] + early_b[rows] + early_x[rows]
+            if first:
+                at = jnp.where(chip == 0, jnp.clip(s, 0, 1), jnp.clip(s, 5, 6) - 3)
+                outer = late[at] + late_b[at] + late_x[at - 2 * chip]
+                main = jnp.where(s == near, main, outer)
+            own = jnp.where(lane == s, column, 0.0)
+            block = jnp.concatenate([main, own], axis=1)
             place(pleft, jnp.concatenate([block, blank], axis=0), i * KROWS, 16)
         kacc[...] = dot(pleft[...], kc[...])
         for i in range(2):
@@ -471,11 +502,17 @@
         pltpu.VMEM((2 * HR, 2 * HC), F32),
         pltpu.VMEM((2 * KROWS, 2 * HC), F32),
         dma(10),
-        pltpu.VMEM((8, SENT, LANES), F32),
-        pltpu.VMEM((3, SENT, LANES), F32),
-        pltpu.VMEM((8, SENT, LANES), F32),
-        pltpu.VMEM((3, SENT, LANES), F32),
-        pltpu.VMEM((6, SENT, LANES), F32),
+        pltpu.VMEM((2 * SHARE, LANES), F32),
+        pltpu.VMEM((SHARE, LANES), F32),
+        pltpu.VMEM((2 * SHARE, LANES), F32),
+        pltpu.VMEM((SHARE, LANES), F32),
+        pltpu.VMEM((2 * SHARE, LANES), F32),
+        pltpu.VMEM((4, SENT, LANES), F32),
+        pltpu.VMEM((SENT, LANES), F32),
+        pltpu.VMEM((4, SENT, LANES), F32),
+        pltpu.VMEM((SENT, LANES), F32),
+        pltpu.VMEM((2, SENT, LANES), F32),
+        pltpu.VMEM((SENT, LANES), F32),
         pltpu.VMEM((2, size // 2, LANES), F32),
         pltpu.VMEM((2, size // 2, LANES), F32),
         pltpu.VMEM((4, B // 2, LANES), F32),

time: 27.8 us -> 27.9 us (level)
  no operation moved by 1% of the time
where the time goes in v5:
time: 27.9 us; the launch traced here: 27.7 us
  Pallas kernels  26.3 us (94%)
  other arithmetic  0.74 us (3%)
  local copies, waits for them, and re-layouts  0.65 us (2%)
    pallas_call x1, Pallas kernels, body(): pl.pallas_call(run, out_shape=(shape, shape), in_specs=[hbm, hbm, hbm, pl...  26.3 us
    add x1, other arithmetic, body(): return kept + received  0.74 us
    unnamed x2, local copies, waits for them, and re-layouts  0.65 us

profile of v5, /device:TPU:0, one launch (start us, length us, event | category | flops | bytes accessed | tf_op | source)
XLA Modules:
  0.0 27.7 jit_solution(16259613592116778103)
XLA Ops:
  0.0 0.0 copy-start
  0.0 0.7 %copy-done = f32[4]{0:T(128)S(1)} copy-done((f32[4]{0:T(128)S(1)}, f32[4]{0:T(128)}, u32[]{:S(2)}) %copy-start) | copy-done | bytes 40
  0.7 26.3 %shard_map.109 = (f32[1,1,256,256]{3,2,1,0:T(8,128)S(1)}, f32[1,1,256,256]{3,2,1,0:T(8,128)S(1)}) custom-call(f32[1,1,256,256]{3,2,1,0:T(8,128)} %args_0_.4, f32[4,1,256,256]{3,2,1,0:T(8,128)} %args_1_.4, f32[4,129,1,129]{3,2,1,0:T(1,128)} %bitcast.1, f32[4]{0:T(128)S(1)} %copy-done, bf16[768,512]{1,0:T(8,128)(2,1)} %constant.14.clone.args_4_, ...), custom_call_target="tpu_custom_call" | custom-call | flops 4000000000 | bytes 8000000 | tf_op jit(solution)/shard_map/pallas_call | solution.py:543
  27.0 0.7 %add.3 = f32[1,1,256,256]{3,2,1,0:T(8,128)} add(f32[1,1,256,256]{3,2,1,0:T(8,128)S(1)} %get-tuple-element.7, f32[1,1,256,256]{3,2,1,0:T(8,128)S(1)} %get-tuple-element.8) | non-fusion elementwise | flops 65536 | bytes 786432 | tf_op jit(solution)/shard_map/add | solution.py:554
Async XLA Ops:
  0.0 0.7 %copy-start = (f32[4]{0:T(128)S(1)}, f32[4]{0:T(128)}, u32[]{:S(2)}) copy-start(f32[4]{0:T(128)} %args_3_.4) | copy-start | bytes 52

commit v6 on v5

--- a/solution.py
+++ b/solution.py
@@ -259,12 +259,13 @@
     a_copies = [to_sib(early.at[piece(i, 1 - core)], early_a.at[piece(i, 0)], i) for i in range(2)]
     a_copies.append(to_sib(late.at[away_late + 1 - core], late_a, 2))
     b_copies = [to_sib(early, early_b, 3), to_sib(late, late_b, 4)]
-    a_copies[0].start()
-    a_copies[1].start()
     for d in sorted(NEIGHBOURS, key=lambda d: abs(d[0]) + abs(d[1]) == 2):
         @pl.when(exists(d))
         def _():
             halo(d).start()
+
+    a_copies[0].start()
+    a_copies[1].start()
 
     x_copies, f_copies = [], []
     for i in range(3):
@@ -319,55 +320,8 @@
     late_sum[...] = late[away_late + core] + late_a[...]
     x_copies[2].start()
 
-    for d in NEIGHBOURS:
-        dr, dc = d
-        there = exists(d)
-        incoming = halo((-dr, -dc))
-
-        @pl.when(there)
-        def _():
-            incoming.wait_recv()
-
-        if dr == 0:
-            ref, i = side_in, (1 - dc) // 2
-        elif dc == 0:
-            ref, i = vert_in, (1 - dr) // 2
-        else:
-            ref, i = corner_in, (1 - dr) + (1 - dc) // 2
-
-        @pl.when(jnp.logical_not(there))
-        def _():
-            ref[i] = jnp.zeros(ref.shape[1:], F32)
-
-    def edge(right, left, m):
-        top = jnp.where(m, right, left)
-        bottom = pltpu.roll(jnp.where(m, left, right), LANES // 2, 1)
-        return jnp.concatenate([top, bottom], axis=0)
-
     def place(ref, x, row, step):
         put_left(ref, lambda rows: x[rows], x.shape[0], row, step)
-
-    place(xe, edge(side_in[0], side_in[1], half_mask((h, LANES))), 0, 64)
-    small = half_mask((B // 2, LANES))
-    for i in range(2):
-        put_left(xo, lambda rows: vert_in[i, rows], B, size + i * B)
-        place(xe, edge(corner_in[2 * i], corner_in[2 * i + 1], small), size + i * B, 64)
-    total_rows = size + 2 * B
-    acc[0:size] = own_part[...] + dot(xe[0:size], fe[...])
-    acc[size:total_rows] = dot(xo[size:], fo[...]) + dot(xe[size:], fe[...])
-    put_right(yr, lambda rows: acc[rows], total_rows, total_rows)
-    acc[...] = dot(fr[...], yr[...])
-
-    def halves(load, rows):
-        below = slice(HR + rows.start, HR + rows.stop)
-        cc, cs = load(rows, slice(0, HC)), load(rows, slice(HC, 2 * HC))
-        sc, ss = load(below, slice(0, HC)), load(below, slice(HC, 2 * HC))
-        return cc - ss, sc + cs, cc + ss, sc - cs
-
-    for r in range(0, HR, 16):
-        rows = slice(r, r + 16)
-        for n, x in enumerate(halves(lambda a, b: acc[a, b], rows)):
-            field[n, rows] = x
 
     def forwarded(i):
         other = early_x.at[piece(i, 1 - core)] if i < 2 else late_x.at[1 - core]
@@ -403,6 +357,58 @@
             )
             kern[i] = dot(kr[...], kright[i])
 
+    forwarded(0)
+    forwarded(1)
+    b_copies[0].wait_recv()
+    kernels(0)
+
+    for d in NEIGHBOURS:
+        dr, dc = d
+        there = exists(d)
+        incoming = halo((-dr, -dc))
+
+        @pl.when(there)
+        def _():
+            incoming.wait_recv()
+
+        if dr == 0:
+            ref, i = side_in, (1 - dc) // 2
+        elif dc == 0:
+            ref, i = vert_in, (1 - dr) // 2
+        else:
+            ref, i = corner_in, (1 - dr) + (1 - dc) // 2
+
+        @pl.when(jnp.logical_not(there))
+        def _():
+            ref[i] = jnp.zeros(ref.shape[1:], F32)
+
+    def edge(right, left, m):
+        top = jnp.where(m, right, left)
+        bottom = pltpu.roll(jnp.where(m, left, right), LANES // 2, 1)
+        return jnp.concatenate([top, bottom], axis=0)
+
+    place(xe, edge(side_in[0], side_in[1], half_mask((h, LANES))), 0, 64)
+    small = half_mask((B // 2, LANES))
+    for i in range(2):
+        put_left(xo, lambda rows: vert_in[i, rows], B, size + i * B)
+        place(xe, edge(corner_in[2 * i], corner_in[2 * i + 1], small), size + i * B, 64)
+    total_rows = size + 2 * B
+    acc[0:size] = own_part[...] + dot(xe[0:size], fe[...])
+    acc[size:total_rows] = dot(xo[size:], fo[...]) + dot(xe[size:], fe[...])
+    put_right(yr, lambda rows: acc[rows], total_rows, total_rows)
+    acc[...] = dot(fr[...], yr[...])
+
+    def halves(load, rows):
+        below = slice(HR + rows.start, HR + rows.stop)
+        cc, cs = load(rows, slice(0, HC)), load(rows, slice(HC, 2 * HC))
+        sc, ss = load(below, slice(0, HC)), load(below, slice(HC, 2 * HC))
+        return cc - ss, sc + cs, cc + ss, sc - cs
+
+    for r in range(0, HR, 16):
+        rows = slice(r, r + 16)
+        for n, x in enumerate(halves(lambda a, b: acc[a, b], rows)):
+            field[n, rows] = x
+
     def term(i, put):
         for r in range(0, HR, 16):
             rows = slice(r, r + 16)
@@ -457,10 +463,6 @@
         pairs[1][j].wait_recv()
         out[0, 0, rows] = value + pair_in[1, rows]
 
-    forwarded(0)
-    forwarded(1)
-    b_copies[0].wait_recv()
-    kernels(0)
     x_copies[2].wait_recv()
     f_copies[2].start()
     term(0, to_pair(0))

time: 27.9 us -> 27.7 us (level)
  no operation moved by 1% of the time
where the time goes in v6:
time: 27.7 us; the launch traced here: 27.5 us
  Pallas kernels  26.1 us (94%)
  other arithmetic  0.74 us (3%)
  local copies, waits for them, and re-layouts  0.65 us (2%)
    pallas_call x1, Pallas kernels, body(): pl.pallas_call(run, out_shape=(shape, shape), in_specs=[hbm, hbm, hbm, pl...  26.1 us
    add x1, other arithmetic, body(): return kept + received  0.74 us
    unnamed x2, local copies, waits for them, and re-layouts  0.65 us

profile of v6, /device:TPU:0, one launch (start us, length us, event | category | flops | bytes accessed | tf_op | source)
XLA Modules:
  0.0 27.5 jit_solution(3409714186032267254)
XLA Ops:
  0.0 0.0 copy-start
  0.0 0.7 %copy-done = f32[4]{0:T(128)S(1)} copy-done((f32[4]{0:T(128)S(1)}, f32[4]{0:T(128)}, u32[]{:S(2)}) %copy-start) | copy-done | bytes 40
  0.7 26.1 %shard_map.109 = (f32[1,1,256,256]{3,2,1,0:T(8,128)S(1)}, f32[1,1,256,256]{3,2,1,0:T(8,128)S(1)}) custom-call(f32[1,1,256,256]{3,2,1,0:T(8,128)} %args_0_.4, f32[4,1,256,256]{3,2,1,0:T(8,128)} %args_1_.4, f32[4,129,1,129]{3,2,1,0:T(1,128)} %bitcast.1, f32[4]{0:T(128)S(1)} %copy-done, bf16[768,512]{1,0:T(8,128)(2,1)} %constant.14.clone.args_4_, ...), custom_call_target="tpu_custom_call" | custom-call | flops 4000000000 | bytes 8000000 | tf_op jit(solution)/shard_map/pallas_call | solution.py:545
  26.8 0.7 %add.3 = f32[1,1,256,256]{3,2,1,0:T(8,128)} add(f32[1,1,256,256]{3,2,1,0:T(8,128)S(1)} %get-tuple-element.7, f32[1,1,256,256]{3,2,1,0:T(8,128)S(1)} %get-tuple-element.8) | non-fusion elementwise | flops 65536 | bytes 786432 | tf_op jit(solution)/shard_map/add | solution.py:556
Async XLA Ops:
  0.0 0.7 %copy-start = (f32[4]{0:T(128)S(1)}, f32[4]{0:T(128)}, u32[]{:S(2)}) copy-start(f32[4]{0:T(128)} %args_3_.4) | copy-start | bytes 52
